TPU v7x, 256 devices: a whole 4x4x8 slice. The times are simulated.
256 devices in a mesh: seq: 32 (over z, y), win: 8 (over x, core).
Axes of the slice: x: 4, y: 4, z: 8, core: 2. Of those that a mesh axis runs over, the one named last changes fastest.
Arguments:
- bases: int32 [8, 8192], P('win', 'seq'), may hold values from 0 to 3
- stem_weight: float32 [20, 768], replicated, may hold values from -3 to 3
- norm_gain: float32 [768], replicated, may hold values from 0.1 to 1.9
- conv_weight: bfloat16 [3840, 768], P(('seq', 'win')), may hold values from -0.09375 to 0.09375
- cotangent: bfloat16 [8, 4096, 768], P('win', 'seq'), may hold values from -0.079589844 to 0.079589844
Outputs:
- conv_grad: float32 [3840, 768], P(('seq', 'win'))
- stem_grad: float32 [20, 768], replicated
- gain_grad: float32 [768], replicated
All inputs are finite; a program needn't handle non-finite values.
Results may differ from a plain program's by a relative error of at most 0.0044.
Values may be sent and summed in bfloat16 or wider, within the bound.
No kernel may reach another device: no remote copies, remote signals or barrier semaphores. Data moves between devices by JAX's collectives and lax.ppermute only.
A program may use at most 64 MiB of HBM per device.

v0:
```python
import jax
import jax.numpy as jnp
from jax import lax
from jax.sharding import PartitionSpec as P

KW = 5


def padded(cells, sides, width):
    for axis, dim in sides:
        count = lax.axis_size(axis)
        ends = count - 1
        head = lax.slice_in_dim(cells, 0, width, axis=dim)
        tail = lax.slice_in_dim(cells, cells.shape[dim] - width, cells.shape[dim], axis=dim)
        cells = jnp.concatenate(
            [
                lax.ppermute(tail, axis, [(i, (i + 1) % count) for i in range(ends)]),
                cells,
                lax.ppermute(head, axis, [((i + 1) % count, i) for i in range(ends)]),
            ],
            axis=dim,
        )
    return cells


def norm_rows(x0, gain):
    scale = lax.rsqrt(jnp.mean(x0 * x0, axis=-1, keepdims=True) + 1e-06)
    return x0 * scale * gain


def gelu_back(pre, upstream):
    return jax.vjp(jax.nn.gelu, pre)[1](upstream)[0]


def stem_rows(bases_ext, first_pos, total, stem_weight):
    count = bases_ext.shape[0] - 4
    places = first_pos + jnp.arange(bases_ext.shape[0], dtype=jnp.int32)
    valid = (places >= 0) & (places < total)
    onehot = (
        (bases_ext[:, None] == jnp.arange(4, dtype=jnp.int32)[None, :]) & valid[:, None]
    ).astype(jnp.float32)
    stem_cols = jnp.concatenate([onehot[t : t + count] for t in range(KW)], axis=1)
    x0 = jnp.dot(
        stem_cols, stem_weight, precision=lax.Precision.HIGHEST, preferred_element_type=jnp.float32
    )
    return (stem_cols, x0)


def shards(bases, stem_weight, norm_gain, conv_weight, cotangent):
    rows = bases.shape[1]
    channels = norm_gain.shape[0]
    total = rows * lax.axis_size("seq")
    offset = lax.axis_index("seq") * rows
    narrow = padded(bases, (("seq", 1),), 2)[0]
    stem_cols, x0 = stem_rows(narrow, offset - 2, total, stem_weight)
    xn = norm_rows(x0, norm_gain).astype(jnp.bfloat16)
    xn_ext = padded(xn[None], (("seq", 1),), 2)[0]
    conv_cols = jnp.concatenate([xn_ext[t : t + rows] for t in range(KW)], axis=1)
    weights = lax.all_gather(conv_weight, ("seq", "win"), axis=0, tiled=True)
    pre = jnp.dot(conv_cols, weights, preferred_element_type=jnp.float32)
    upstream = 0.5 * jnp.repeat(cotangent[0].astype(jnp.float32), 2, axis=0)
    dpre = gelu_back(pre, upstream).astype(jnp.bfloat16)
    conv_grad = lax.psum_scatter(
        lax.dot_general(
            conv_cols, dpre, (((0,), (0,)), ((), ())), preferred_element_type=jnp.float32
        ),
        ("seq", "win"),
        scatter_dimension=0,
        tiled=True,
    )
    dpre_ext = padded(dpre[None], (("seq", 1),), 2)[0]
    dxn = jnp.zeros((rows, channels), jnp.float32)
    for t in range(KW):
        tap_rows = weights[t * channels : (t + 1) * channels]
        dxn = dxn + lax.dot_general(
            dpre_ext[4 - t : 4 - t + rows],
            tap_rows,
            (((1,), (1,)), ((), ())),
            preferred_element_type=jnp.float32,
        )
    back = jax.vjp(norm_rows, x0, norm_gain)[1](dxn)
    dx0 = upstream + back[0]
    stem_local = lax.dot_general(
        stem_cols,
        dx0,
        (((0,), (0,)), ((), ())),
        precision=lax.Precision.HIGHEST,
        preferred_element_type=jnp.float32,
    )
    stem_grad, gain_grad = lax.psum((stem_local, back[1]), ("seq", "win"))
    return (conv_grad, stem_grad, gain_grad)


def solution(mesh):
    in_specs = (P("win", "seq"), P(), P(), P(("seq", "win"), None), P("win", "seq", None))
    out_specs = (P(("seq", "win"), None), P(), P())
    return jax.shard_map(shards, mesh=mesh, in_specs=in_specs, out_specs=out_specs, check_vma=False)
```

profile of v0, /device:TPU:1, one launch (start us, length us, event | category | flops | bytes accessed | tf_op | source)
XLA Modules:
  0.0 1010.2 jit_solution(404550902734466600)
XLA Ops:
  8.7 4.0 collective-permute-start
  12.7 1.3 collective-permute-start.1
  14.0 3.0 collective-permute-done.1
  19.7 3.2 collective-permute-start.2
  23.2 1.5 mul.123
  26.4 2.7 collective-permute-done.3
  29.3 102.7 %all-gather.3.cloned.1.call-done = bf16[256,15,768]{2,1,0:T(8,128)(2,1)} async-done(((bf16[1,15,768]{2,1,0:T(8,128)(2,1)}), bf16[256,15,768]{2,1,0:T(8,128)(2,1)}) %all-gather.3.cloned.1.call-update) | async-done | bytes 5898256 | tf_op jit(solution)/shard_map/all_gather | solution.py:59
  131.9 9.6 reshape.53
  141.5 4.9 fusion.13
  146.4 6.1 fusion.60
  152.5 1.3 collective-permute-start.4
  153.8 691.9 %fusion = f32[16,768]{1,0:T(8,128)S(1)} fusion(f32[3840,768]{1,0:T(8,128)} %fusion.60), kind=kCustom, calls=%all-reduce-scatter | all-reduce-scatter fusion | flops 3145729 | bytes 11845632
  845.7 1.3 collective-permute-start.20
  847.0 1.3 collective-permute-start.19
  848.3 1.3 collective-permute-start.18
  852.2 1.8 fusion.4
  854.0 1.8 convolution_add_fusion.3
  855.8 1.8 convolution_add_fusion.2
  858.9 1.8 convolution_add_fusion.1
  860.8 1.4 collective-permute-start.16
  862.2 2.0 multiply_reduce_fusion
  864.2 1.3 collective-permute-start.15
  866.8 6.3 collective-permute-start.13
  873.1 15.7 %collective-permute-start.12 = (f32[16,768]{1,0:T(8,128)S(1)}, f32[16,768]{1,0:T(8,128)S(1)}, u32[]{:S(2)}, u32[]{:S(2)}) collective-permute-start(f32[16,768]{1,0:T(8,128)S(1)} %fusion), channel_id=1, source_target_pairs={{0,7},{1,8},{2,9},{3,10},{4,11},{5,12},{6,13},{7,14},{8,15},{9,16}... | collective-permute-start | bytes 147464
  888.8 12.5 %collective-permute-start.11 = (f32[16,768]{1,0:T(8,128)S(1)}, f32[16,768]{1,0:T(8,128)S(1)}, u32[]{:S(2)}, u32[]{:S(2)}) collective-permute-start(f32[16,768]{1,0:T(8,128)S(1)} %fusion), channel_id=1, source_target_pairs={{0,6},{1,7},{2,8},{3,9},{4,10},{5,11},{6,12},{7,13},{8,14},{9,15},... | collective-permute-start | bytes 147464
  901.3 9.4 collective-permute-start.10
  910.7 3.1 collective-permute-start.9
  913.8 4.0 collective-permute-start.8
  917.8 6.1 collective-permute-start.7
  923.9 1.9 collective-permute-start.6
  926.6 74.0 %all-reduce.2 = (f32[20,768]{1,0:T(8,128)}, f32[768]{0:T(1024)}) all-reduce(f32[20,768]{1,0:T(8,128)S(1)} %fusion.15, f32[768]{0:T(1024)S(1)} %get-tuple-element.3), channel_id=1, replica_groups=mesh['seq'=32,'win'=8] {'seq','win'}, use_global_device_ids=true, to_apply=%region_3.0 | all-reduce | flops 16128 | bytes 129024 | tf_op jit(solution)/shard_map/psum | solution.py:90
  1000.7 2.1 concatenate.34
  (57 shorter events, 12.9 us)
Async XLA Ops:
  7.2 10.7 %copy-start = (f32[20,768]{1,0:T(8,128)S(1)}, f32[20,768]{1,0:T(8,128)}, u32[]{:S(2)}) copy-start(f32[20,768]{1,0:T(8,128)} %param.6) | copy-start | bytes 184324
  7.2 15.7 %copy-start.2 = (bf16[1,128,768]{2,1,0:T(8,128)(2,1)S(1)}, bf16[1,128,768]{2,1,0:T(8,128)(2,1)}, u32[]{:S(2)}) copy-start(bf16[1,128,768]{2,1,0:T(8,128)(2,1)} %param.9) | copy-start | bytes 589828
  7.2 124.7 %all-gather.3.cloned.1.call-start = ((), (), s32[]{:S(2)}) async-start(), calls=%async_computation | async-start | bytes 6316032 | tf_op jit(solution)/shard_map/all_gather | solution.py:59
  8.7 5.3 collective-permute-start
  12.7 4.3 collective-permute-start.1
  19.7 6.3 collective-permute-start.2
  22.9 3.3 copy-start.3
  24.7 4.3 collective-permute-start.3
  152.5 698.4 %collective-permute-start.4 = (bf16[1,2,768]{2,1,0:T(2,128)(2,1)S(1)}, bf16[1,2,768]{2,1,0:T(2,128)(2,1)S(1)}, u32[]{:S(2)}, u32[]{:S(2)}) collective-permute-start(bf16[1,2,768]{2,1,0:T(2,128)(2,1)S(1)} %get-tuple-element.8), channel_id=1, source_target_pairs={{8,0},{16,8},{24,16},{32,24},{40,32},{48,40},{56,48},{64,56},{72,6... | collective-permute-start | bytes 9224 | tf_op jit(solution)/shard_map/ppermute | solution.py:19
  845.7 18.5 %collective-permute-start.20 = (f32[16,768]{1,0:T(8,128)S(1)}, f32[16,768]{1,0:T(8,128)S(1)}, u32[]{:S(2)}, u32[]{:S(2)}) collective-permute-start(f32[16,768]{1,0:T(8,128)S(1)} %fusion), channel_id=1, source_target_pairs={{0,15},{1,16},{2,17},{3,18},{4,19},{5,20},{6,21},{7,22},{8,23},{9,... | collective-permute-start | bytes 147464
  847.0 18.5 %collective-permute-start.19 = (f32[16,768]{1,0:T(8,128)S(1)}, f32[16,768]{1,0:T(8,128)S(1)}, u32[]{:S(2)}, u32[]{:S(2)}) collective-permute-start(f32[16,768]{1,0:T(8,128)S(1)} %fusion), channel_id=1, source_target_pairs={{0,14},{1,15},{2,16},{3,17},{4,18},{5,19},{6,20},{7,21},{8,22},{9,... | collective-permute-start | bytes 147464
  848.3 18.5 %collective-permute-start.18 = (f32[16,768]{1,0:T(8,128)S(1)}, f32[16,768]{1,0:T(8,128)S(1)}, u32[]{:S(2)}, u32[]{:S(2)}) collective-permute-start(f32[16,768]{1,0:T(8,128)S(1)} %fusion), channel_id=1, source_target_pairs={{0,13},{1,14},{2,15},{3,16},{4,17},{5,18},{6,19},{7,20},{8,21},{9,... | collective-permute-start | bytes 147464
  849.6 23.5 %collective-permute-start.17 = (f32[16,768]{1,0:T(8,128)S(1)}, f32[16,768]{1,0:T(8,128)S(1)}, u32[]{:S(2)}, u32[]{:S(2)}) collective-permute-start(f32[16,768]{1,0:T(8,128)S(1)} %fusion), channel_id=1, source_target_pairs={{0,12},{1,13},{2,14},{3,15},{4,16},{5,17},{6,18},{7,19},{8,20},{9,... | collective-permute-start | bytes 147464
  850.9 6.7 collective-permute-start.5
  857.6 3.1 collective-permute-start.21
  860.7 65.1 %copy-start.1 = (f32[256,768]{1,0:T(8,128)S(1)}, f32[256,768]{1,0:T(8,128)}, u32[]{:S(2)}) copy-start(f32[256,768]{1,0:T(8,128)} %mul.123) | copy-start | bytes 2359300
  860.8 28.0 %collective-permute-start.16 = (f32[16,768]{1,0:T(8,128)S(1)}, f32[16,768]{1,0:T(8,128)S(1)}, u32[]{:S(2)}, u32[]{:S(2)}) collective-permute-start(f32[16,768]{1,0:T(8,128)S(1)} %fusion), channel_id=1, source_target_pairs={{0,11},{1,12},{2,13},{3,14},{4,15},{5,16},{6,17},{7,18},{8,19},{9,... | collective-permute-start | bytes 147464
  864.2 37.1 %collective-permute-start.15 = (f32[16,768]{1,0:T(8,128)S(1)}, f32[16,768]{1,0:T(8,128)S(1)}, u32[]{:S(2)}, u32[]{:S(2)}) collective-permute-start(f32[16,768]{1,0:T(8,128)S(1)} %fusion), channel_id=1, source_target_pairs={{0,10},{1,11},{2,12},{3,13},{4,14},{5,15},{6,16},{7,17},{8,18},{9,... | collective-permute-start | bytes 147464
  865.5 45.3 %collective-permute-start.14 = (f32[16,768]{1,0:T(8,128)S(1)}, f32[16,768]{1,0:T(8,128)S(1)}, u32[]{:S(2)}, u32[]{:S(2)}) collective-permute-start(f32[16,768]{1,0:T(8,128)S(1)} %fusion), channel_id=1, source_target_pairs={{0,9},{1,10},{2,11},{3,12},{4,13},{5,14},{6,15},{7,16},{8,17},{9,1... | collective-permute-start | bytes 147464
  866.8 47.1 %collective-permute-start.13 = (f32[16,768]{1,0:T(8,128)S(1)}, f32[16,768]{1,0:T(8,128)S(1)}, u32[]{:S(2)}, u32[]{:S(2)}) collective-permute-start(f32[16,768]{1,0:T(8,128)S(1)} %fusion), channel_id=1, source_target_pairs={{0,8},{1,9},{2,10},{3,11},{4,12},{5,13},{6,14},{7,15},{8,16},{9,17... | collective-permute-start | bytes 147464
  873.1 44.7 %collective-permute-start.12 = (f32[16,768]{1,0:T(8,128)S(1)}, f32[16,768]{1,0:T(8,128)S(1)}, u32[]{:S(2)}, u32[]{:S(2)}) collective-permute-start(f32[16,768]{1,0:T(8,128)S(1)} %fusion), channel_id=1, source_target_pairs={{0,7},{1,8},{2,9},{3,10},{4,11},{5,12},{6,13},{7,14},{8,15},{9,16}... | collective-permute-start | bytes 147464
  888.8 35.2 %collective-permute-start.11 = (f32[16,768]{1,0:T(8,128)S(1)}, f32[16,768]{1,0:T(8,128)S(1)}, u32[]{:S(2)}, u32[]{:S(2)}) collective-permute-start(f32[16,768]{1,0:T(8,128)S(1)} %fusion), channel_id=1, source_target_pairs={{0,6},{1,7},{2,8},{3,9},{4,10},{5,11},{6,12},{7,13},{8,14},{9,15},... | collective-permute-start | bytes 147464
  901.3 99.3 %collective-permute-start.10 = (f32[16,768]{1,0:T(8,128)S(1)}, f32[16,768]{1,0:T(8,128)S(1)}, u32[]{:S(2)}, u32[]{:S(2)}) collective-permute-start(f32[16,768]{1,0:T(8,128)S(1)} %fusion), channel_id=1, source_target_pairs={{0,5},{1,6},{2,7},{3,8},{4,9},{5,10},{6,11},{7,12},{8,13},{9,14},{... | collective-permute-start | bytes 147464
  910.7 89.9 %collective-permute-start.9 = (f32[16,768]{1,0:T(8,128)S(1)}, f32[16,768]{1,0:T(8,128)S(1)}, u32[]{:S(2)}, u32[]{:S(2)}) collective-permute-start(f32[16,768]{1,0:T(8,128)S(1)} %fusion), channel_id=1, source_target_pairs={{0,4},{1,5},{2,6},{3,7},{4,8},{5,9},{6,10},{7,11},{8,12},{9,13},{1... | collective-permute-start | bytes 147464
  913.8 86.8 %collective-permute-start.8 = (f32[16,768]{1,0:T(8,128)S(1)}, f32[16,768]{1,0:T(8,128)S(1)}, u32[]{:S(2)}, u32[]{:S(2)}) collective-permute-start(f32[16,768]{1,0:T(8,128)S(1)} %fusion), channel_id=1, source_target_pairs={{0,3},{1,4},{2,5},{3,6},{4,7},{5,8},{6,9},{7,10},{8,11},{9,12},{10... | collective-permute-start | bytes 147464
  917.8 82.8 %collective-permute-start.7 = (f32[16,768]{1,0:T(8,128)S(1)}, f32[16,768]{1,0:T(8,128)S(1)}, u32[]{:S(2)}, u32[]{:S(2)}) collective-permute-start(f32[16,768]{1,0:T(8,128)S(1)} %fusion), channel_id=1, source_target_pairs={{0,2},{1,3},{2,4},{3,5},{4,6},{5,7},{6,8},{7,9},{8,10},{9,11},{10,... | collective-permute-start | bytes 147464
  923.9 76.7 %collective-permute-start.6 = (f32[16,768]{1,0:T(8,128)S(1)}, f32[16,768]{1,0:T(8,128)S(1)}, u32[]{:S(2)}, u32[]{:S(2)}) collective-permute-start(f32[16,768]{1,0:T(8,128)S(1)} %fusion), channel_id=1, source_target_pairs={{0,1},{1,2},{2,3},{3,4},{4,5},{5,6},{6,7},{7,8},{8,9},{9,10},{10,1... | collective-permute-start | bytes 147464
Sparse Core Ops, SparseCore 0:
  11.8 120.1 all-gather.2
where the time goes:
time: 1010 us
  blocking collectives  766 us (76%)
  waiting for transfers between devices  109 us (11%)
  starting transfers between devices  81.8 us (8%)
  matrix products  21.8 us (2%)
  local copies, waits for them, and re-layouts  15 us (1%)
  between operations  14.6 us (1%)
    unnamed x1, blocking collectives  692 us
    all_gather x1, waiting for transfers between devices, shards(): weights = lax.all_gather(conv_weight, ('seq', 'win'), axis=0, tiled=True)  103 us
    psum x1, blocking collectives, shards(): stem_grad, gain_grad = lax.psum((stem_local, back[1]), ('seq', 'win'))  74 us
    unnamed x16, starting transfers between devices  69.4 us
  transfers between devices with their start and end apart: 23, of which 3 were waited for; matrix products, arithmetic and copies ran while one was open for 70% of the time, Pallas kernels for 0%

commit v1 on v0

v1 whole, which is shorter than its diff:
```python
import functools

import jax
import jax.numpy as jnp
from jax import lax
from jax.experimental import pallas as pl
from jax.experimental.pallas import tpu as pltpu
from jax.sharding import PartitionSpec as P

KW = 5
AXES = ("seq", "win")
F32 = jnp.float32
BF16 = jnp.bfloat16
HIGH = lax.Precision.HIGHEST
ROOT = 0.7978845608028654
CUBE = 0.044715


def pieces(x, count):
    out = []
    for _ in range(count):
        top = x.astype(BF16)
        out.append(top)
        x = x - top.astype(F32)
    return out


def gelu_slope(x):
    sq = x * x
    th = jnp.tanh(ROOT * x * (1.0 + CUBE * sq))
    return 0.5 * (1.0 + th) + (0.5 * ROOT) * x * (1.0 - th * th) * (1.0 + 3.0 * CUBE * sq)


def main_kernel(channels, sym_ref, dr_ref, table_ref, out_ref):
    lanes = dr_ref.shape[-1]
    lane = lax.broadcasted_iota(jnp.int32, (8, lanes), 1)
    sub = lax.broadcasted_iota(jnp.int32, (8, lanes), 0)
    top = sub < 4
    first, last = lane == 0, lane == lanes - 1
    base = (sub % 4).astype(F32)

    def down(x, fill):
        return jnp.where(first, fill, pltpu.roll(x, 1, 1))

    def up(x, fill):
        return jnp.where(last, fill, pltpu.roll(x, lanes - 1, 1))

    table = table_ref[...]

    def window(w, total):
        sym = sym_ref[w]
        mid = jnp.where(top, sym[0:1], sym[1:2])
        hot = [
            (cell == base).astype(F32) for cell in (down(mid, -1.0), mid, up(mid, -1.0))
        ]
        hots = jnp.concatenate(hot, axis=0)
        narrow = hots.astype(BF16)
        looked = jnp.dot(
            table, jnp.concatenate([narrow] * 3, axis=0), preferred_element_type=F32
        )
        taps = [looked[8 * t : 8 * t + 8] for t in range(KW)]
        mean_e = jnp.sum(looked[40:64] * hots, axis=0, keepdims=True)
        mean_o = jnp.sum(looked[64:88] * hots, axis=0, keepdims=True)
        scale_e = lax.rsqrt(mean_e + 1e-06)
        scale_o = lax.rsqrt(mean_o + 1e-06)
        scale = jnp.where(top, scale_e, scale_o)
        swapped = jnp.where(top, scale_o, scale_e)
        p0, p2, p4 = taps[0] * scale, taps[2] * scale, taps[4] * scale
        p1, p3 = taps[1] * swapped, taps[3] * swapped
        pre = down(p0 + jnp.where(top, p1, 0.0), 0.0)
        pre = pre + p2 + jnp.where(top, p3, p1)
        pre = pre + up(p4 + jnp.where(top, 0.0, p3), 0.0)
        dr = dr_ref[w].astype(F32)
        dpre = dr * gelu_slope(pre)
        ahead, behind = up(dpre, 0.0), down(dpre, 0.0)
        d1 = jnp.where(top, ahead, dpre)
        d3 = jnp.where(top, dpre, behind)
        here = taps[0] * ahead + taps[2] * dpre + taps[4] * behind
        there = taps[1] * d1 + taps[3] * d3
        both = here + pltpu.roll(there, 4, 0)
        q_e = jnp.sum(jnp.where(top, both, 0.0), axis=0, keepdims=True)
        q_o = jnp.sum(jnp.where(top, 0.0, both), axis=0, keepdims=True)
        u_e = q_e * scale_e * scale_e * scale_e * (1.0 / channels)
        u_o = q_o * scale_o * scale_o * scale_o * (1.0 / channels)
        rows = [ahead * scale, d1 * swapped, dpre * scale, d3 * swapped, behind * scale, dr]
        rows = jnp.concatenate(rows + [hots * u_e, hots * u_o], axis=0)
        found = jnp.zeros((rows.shape[0], 24), F32)
        for part in pieces(rows, 2):
            found = found + lax.dot_general(
                part, narrow, (((1,), (1,)), ((), ())), preferred_element_type=F32
            )
        return total + found

    out_ref[...] = lax.fori_loop(
        0, sym_ref.shape[0], window, jnp.zeros(out_ref.shape, F32)
    )


def main_call(channels, sym, dr, table):
    return pl.pallas_call(
        functools.partial(main_kernel, channels),
        out_shape=jax.ShapeDtypeStruct((96, 24), F32),
        in_specs=[pl.BlockSpec(memory_space=pltpu.VMEM)] * 3,
        out_specs=pl.BlockSpec(memory_space=pltpu.VMEM),
        compiler_params=pltpu.CompilerParams(vmem_limit_bytes=40 * 1024 * 1024),
    )(sym, dr, table)


def exchange(x):
    return lax.all_to_all(x, AXES, 0, 0, tiled=True)


def shards(bases, stem_weight, norm_gain, conv_weight, cotangent):
    seq, win = lax.axis_size("seq"), lax.axis_size("win")
    n = seq * win
    channels = norm_gain.shape[0]
    cols = channels // n
    half = bases.shape[1] // 2
    share = conv_weight.shape[0]
    taps = 4 * KW

    cot = cotangent[0].reshape(half, cols, n).transpose(2, 1, 0)
    own = conv_weight.reshape(share, cols, n).transpose(2, 1, 0)
    even_odd = bases[0].reshape(half, 2).T.astype(BF16)
    sent = jnp.concatenate(
        [
            cot.reshape(n, cols * half),
            jnp.broadcast_to(even_odd.reshape(1, 2 * half), (n, 2 * half)),
            own.reshape(n, cols * share),
        ],
        axis=1,
    )
    got = exchange(sent)
    cot = got[:, : cols * half].reshape(seq, win, cols, half).transpose(1, 2, 0, 3)
    cot = cot.reshape(win, cols, seq * half)
    dr = jnp.pad(0.5 * cot, ((0, 0), (0, 4 - cols), (0, 0)))
    dr = jnp.concatenate([dr, dr], axis=1)
    sym = got[:, cols * half : (cols + 2) * half].reshape(seq, win, 2, half)
    sym = sym.transpose(1, 2, 0, 3).reshape(win, 2, seq * half).astype(F32)
    weights = got[:, (cols + 2) * half :].reshape(n, cols, share)
    weights = weights.transpose(1, 0, 2).reshape(cols, KW, channels).astype(F32)

    gained = stem_weight * norm_gain
    mixed = jnp.einsum("kc,mtc->tmk", gained, weights, precision=HIGH)
    gram = jnp.dot(stem_weight, stem_weight.T, precision=HIGH) * (1.0 / channels)
    even = jnp.pad(mixed, ((0, 0), (0, 4 - cols), (0, 4)))
    odd = jnp.pad(mixed, ((0, 0), (0, 4 - cols), (4, 0)))
    swap = (jnp.arange(KW) % 2 == 1)[:, None, None]
    table = jnp.concatenate(
        [jnp.where(swap, odd, even), jnp.where(swap, even, odd)], axis=1
    ).reshape(8 * KW, 24)
    table = jnp.concatenate(
        [table, jnp.pad(gram, ((0, 4), (0, 4))), jnp.pad(gram, ((4, 0), (4, 0)))], axis=0
    )
    table = jnp.concatenate(pieces(table, 3), axis=1)

    found = main_call(channels, sym, dr, table)

    sums = found[:48].reshape(6, 2, 4, 24)[:, :, :cols]
    swap = jnp.concatenate([swap, swap[:1]], axis=0)
    sums = jnp.where(
        swap,
        sums[:, 0, :, 4:] + sums[:, 1, :, :taps],
        sums[:, 0, :, :taps] + sums[:, 1, :, 4:],
    )
    grads, direct = sums[:KW], sums[KW]
    crossed = found[48 : 48 + taps, :taps] + found[76:96, 4:]
    conv_rows = jnp.einsum("tmk,kc->mtc", grads, gained, precision=HIGH)
    conv_rows = conv_rows.reshape(cols, n, share).transpose(1, 2, 0).reshape(n, share * cols)
    back = jnp.einsum("tmk,mtc->kc", grads, weights, precision=HIGH)
    stem_part = norm_gain * back - jnp.dot(crossed, stem_weight, precision=HIGH)
    gain_part = jnp.sum(stem_weight * back, axis=0, keepdims=True)
    small = jnp.concatenate([stem_part, gain_part], axis=0)
    small = small.reshape(taps + 1, cols, n).transpose(2, 0, 1).reshape(n, (taps + 1) * cols)
    got = exchange(jnp.concatenate([conv_rows, small], axis=1))
    conv_grad = got[:, : share * cols].T.reshape(share, channels)
    mine = jnp.sum(got[:, share * cols :], axis=0)
    mine = mine + jnp.pad(direct.T, ((0, 1), (0, 0))).reshape(-1)
    full = exchange(jnp.broadcast_to(mine[None], (n, mine.shape[0])))
    full = full.T.reshape(taps + 1, channels)
    return (conv_grad, full[:taps], full[taps])


def solution(mesh):
    in_specs = (P("win", "seq"), P(), P(), P(("seq", "win"), None), P("win", "seq", None))
    out_specs = (P(("seq", "win"), None), P(), P())
    return jax.shard_map(shards, mesh=mesh, in_specs=in_specs, out_specs=out_specs, check_vma=False)
```

time: 1010 us -> 104 us (0.10)
  blocking collectives: 766 us -> 0 us
  waiting for transfers between devices: 109 us -> 49.9 us
  starting transfers between devices: 81.8 us -> 27.5 us
  matrix products: 21.8 us -> 1.09 us
  between operations: 14.6 us -> 1 us
  Pallas kernels: 0 us -> 11.3 us
    unnamed x1 -> x0, blocking collectives: 692 us -> none
    all_gather x1 -> x0, waiting for transfers between devices: 103 us -> none  [shards(): weights = lax.all_gather(conv_weight, ('seq', 'win'), axis=0, tiled=True)]
    psum x1 -> x0, blocking collectives: 74 us -> none  [shards(): stem_grad, gain_grad = lax.psum((stem_local, back[1]), ('seq', 'win'))]
    unnamed x16 -> x0, starting transfers between devices: 69.4 us -> none
    all_to_all x0 -> x3, waiting for transfers between devices: none -> 49.9 us  [exchange(): return lax.all_to_all(x, AXES, 0, 0, tiled=True)]
    all_to_all x0 -> x3, starting transfers between devices: none -> 27.5 us  [exchange(): return lax.all_to_all(x, AXES, 0, 0, tiled=True)]
    dot_general x9 -> x5, matrix products: 21.8 us -> 1.09 us  [the longest x1 0.27 us: shards(): stem_part = norm_gain * back - jnp.dot(crossed, stem_weight, precision=HIGH)]
    ppermute x6 -> x0, starting transfers between devices: 12.4 us -> none  [the longest x3 8.51 us: padded(): lax.ppermute(tail, axis, [(i, (i + 1) % count) for i in range(ends)])]
  transfers between devices with their start and end apart: 23 -> 3, of which waited for: 3 -> 3; matrix products, arithmetic and copies ran while one was open for 70% -> 1% of each run, Pallas kernels for 0% -> 0%
where the time goes in v1:
time: 104 us
  waiting for transfers between devices  49.9 us (48%)
  starting transfers between devices  27.5 us (26%)
  local copies, waits for them, and re-layouts  11.7 us (11%)
  Pallas kernels  11.3 us (11%)
  other arithmetic  1.15 us (1%)
  matrix products  1.09 us (1%)
    all_to_all x3, waiting for transfers between devices, exchange(): return lax.all_to_all(x, AXES, 0, 0, tiled=True)  49.9 us
    all_to_all x3, starting transfers between devices, exchange(): return lax.all_to_all(x, AXES, 0, 0, tiled=True)  27.5 us
    pallas_call x1, Pallas kernels, main_call(): pl.pallas_call(functools.partial(main_kernel, channels), out_shape=jax.Sh...  11.3 us
    all_to_all x3, local copies, waits for them, and re-layouts, exchange(): return lax.all_to_all(x, AXES, 0, 0, tiled=True)  3.46 us
    unnamed x11, local copies, waits for them, and re-layouts  2.78 us
  transfers between devices with their start and end apart: 3, of which 3 were waited for; matrix products, arithmetic and copies ran while one was open for 1% of the time, Pallas kernels for 0%

profile of v1, /device:TPU:1, one launch (start us, length us, event | category | flops | bytes accessed | tf_op | source)
XLA Modules:
  0.0 103.6 jit_solution(10712061063204555574)
XLA Ops:
  0.6 1.1 %copy.102 = bf16[1,128,768]{1,2,0:T(8,128)(2,1)S(1)} copy(bf16[1,128,768]{2,1,0:T(8,128)(2,1)} %param.9) | data formatting | bytes 393216 | tf_op args[4]
  1.7 0.1 copy.103
  1.9 0.6 copy-done.2
  2.5 0.6 copy-done.3
  3.2 0.2 convert_element_type.47
  3.5 0.2 maximum_bitcast_fusion
  3.6 1.9 %copy.106 = bf16[256,1,685]{2,1,0:T(2,128)(2,1)} copy(bf16[256,1,685]{0,2,1:T(8,128)(2,1)S(1)} %maximum_bitcast_fusion) | data formatting | bytes 701440 | tf_op jit(solution)/shard_map/all_to_all | solution.py:110
  5.5 15.7 %all-to-all-start = ((bf16[256,1,685]{2,1,0:T(2,128)(2,1)}), bf16[256,1,685]{2,1,0:T(2,128)(2,1)S(1)}, u32[]{:S(2)}, u32[]{:S(2)}) async-start(bf16[256,1,685]{2,1,0:T(2,128)(2,1)} %copy.106), calls=%async_computation | async-start | bytes 1572864 | tf_op jit(solution)/shard_map/all_to_all | solution.py:110
  21.3 0.2 convolution_multiply_fusion
  21.5 24.7 %all-to-all-done = bf16[256,1,685]{2,1,0:T(2,128)(2,1)S(1)} async-done(((bf16[256,1,685]{2,1,0:T(2,128)(2,1)}), bf16[256,1,685]{2,1,0:T(2,128)(2,1)S(1)}, u32[]{:S(2)}, u32[]{:S(2)}) %all-to-all-start) | async-done | bytes 350752 | tf_op jit(solution)/shard_map/all_to_all | solution.py:110
  46.2 0.8 copy.107
  47.1 0.2 copy.113
  47.3 0.3 reshape.116
  47.6 0.3 copy-done.1
  48.0 0.2 convolution_bitcast_fusion.2
  48.5 0.2 copy.110
  48.9 0.2 pad_maximum_fusion.dr_ref
  49.6 11.3 %shard_map.76 = f32[96,24]{1,0:T(8,128)S(1)} custom-call(f32[8,2,4096]{2,1,0:T(2,128)S(1)} %reshape.124.sym_ref, bf16[8,8,4096]{2,1,0:T(8,128)(2,1)S(1)} %pad_maximum_fusion.dr_ref, bf16[88,72]{1,0:T(8,128)(2,1)S(1)} %pad_maximum_fusion.2.table_ref), custom_call_target="tpu_custom_call" | custom-call | tf_op jit(solution)/shard_map/pallas_call | solution.py:100
  61.1 0.2 convolution_bitcast_fusion.1
  61.3 0.2 multiply_reduce_fusion
  61.5 0.3 reshape.119
  61.8 0.2 copy.120
  62.1 0.3 convolution_subtract_fusion
  62.5 0.7 copy.121
  63.3 6.4 %all-to-all-start.1 = ((f32[256,1,108]{2,1,0:T(1,128)}), f32[256,1,108]{2,1,0:T(1,128)S(1)}, u32[]{:S(2)}, u32[]{:S(2)}) async-start(f32[256,1,108]{2,1,0:T(1,128)} %copy.121), calls=%async_computation.1 | async-start | bytes 262144 | tf_op jit(solution)/shard_map/all_to_all | solution.py:110
  69.9 12.8 %all-to-all-done.1 = f32[256,1,108]{2,1,0:T(1,128)S(1)} async-done(((f32[256,1,108]{2,1,0:T(1,128)}), f32[256,1,108]{2,1,0:T(1,128)S(1)}, u32[]{:S(2)}, u32[]{:S(2)}) %all-to-all-start.1) | async-done | bytes 110624 | tf_op jit(solution)/shard_map/all_to_all | solution.py:110
  82.8 0.7 broadcast_in_dim.45
  83.5 5.4 %all-to-all-start.2 = ((f32[256,1,63]{2,1,0:T(1,128)}), f32[256,1,63]{2,1,0:T(1,128)S(1)}, u32[]{:S(2)}, u32[]{:S(2)}) async-start(f32[256,1,63]{2,1,0:T(1,128)} %broadcast_in_dim.45), calls=%async_computation.2 | async-start | bytes 262144 | tf_op jit(solution)/shard_map/all_to_all | solution.py:110
  89.1 0.6 reshape.122
  89.7 12.4 %all-to-all-done.2 = f32[256,1,63]{2,1,0:T(1,128)S(1)} async-done(((f32[256,1,63]{2,1,0:T(1,128)}), f32[256,1,63]{2,1,0:T(1,128)S(1)}, u32[]{:S(2)}, u32[]{:S(2)}) %all-to-all-start.2) | async-done | bytes 64544 | tf_op jit(solution)/shard_map/all_to_all | solution.py:110
  102.3 0.7 slice.80
  103.0 0.6 squeeze.5
  (51 shorter events, 2.2 us)
Async XLA Ops:
  1.7 0.7 copy-start.2
  2.5 0.7 copy-start.3
  5.5 15.8 %copy-start = (f32[20,768]{1,0:T(8,128)S(1)}, f32[20,768]{1,0:T(8,128)}, u32[]{:S(2)}) copy-start(f32[20,768]{1,0:T(8,128)} %param.6) | copy-start | bytes 184324
  5.5 40.7 %all-to-all-start = ((bf16[256,1,685]{2,1,0:T(2,128)(2,1)}), bf16[256,1,685]{2,1,0:T(2,128)(2,1)S(1)}, u32[]{:S(2)}, u32[]{:S(2)}) async-start(bf16[256,1,685]{2,1,0:T(2,128)(2,1)} %copy.106), calls=%async_computation | async-start | bytes 1572864 | tf_op jit(solution)/shard_map/all_to_all | solution.py:110
  47.3 0.7 copy-start.1
  63.3 19.4 %all-to-all-start.1 = ((f32[256,1,108]{2,1,0:T(1,128)}), f32[256,1,108]{2,1,0:T(1,128)S(1)}, u32[]{:S(2)}, u32[]{:S(2)}) async-start(f32[256,1,108]{2,1,0:T(1,128)} %copy.121), calls=%async_computation.1 | async-start | bytes 262144 | tf_op jit(solution)/shard_map/all_to_all | solution.py:110
  83.5 18.6 %all-to-all-start.2 = ((f32[256,1,63]{2,1,0:T(1,128)}), f32[256,1,63]{2,1,0:T(1,128)S(1)}, u32[]{:S(2)}, u32[]{:S(2)}) async-start(f32[256,1,63]{2,1,0:T(1,128)} %broadcast_in_dim.45), calls=%async_computation.2 | async-start | bytes 262144 | tf_op jit(solution)/shard_map/all_to_all | solution.py:110

commit v2 on v1

--- a/solution.py
+++ b/solution.py
@@ -84,16 +84,15 @@
         u_o = q_o * scale_o * scale_o * scale_o * (1.0 / channels)
         rows = [ahead * scale, d1 * swapped, dpre * scale, d3 * swapped, behind * scale, dr]
         rows = jnp.concatenate(rows + [hots * u_e, hots * u_o], axis=0)
-        found = jnp.zeros((rows.shape[0], 24), F32)
-        for part in pieces(rows, 2):
-            found = found + lax.dot_general(
-                part, narrow, (((1,), (1,)), ((), ())), preferred_element_type=F32
-            )
+        found = lax.dot_general(
+            rows.astype(BF16), narrow, (((1,), (1,)), ((), ())), preferred_element_type=F32
+        )
         return total + found
 
-    out_ref[...] = lax.fori_loop(
-        0, sym_ref.shape[0], window, jnp.zeros(out_ref.shape, F32)
-    )
+    total = jnp.zeros(out_ref.shape, F32)
+    for w in range(sym_ref.shape[0]):
+        total = window(w, total)
+    out_ref[...] = total
 
 
 def main_call(channels, sym, dr, table):
@@ -121,23 +120,24 @@
 
     cot = cotangent[0].reshape(half, cols, n).transpose(2, 1, 0)
     own = conv_weight.reshape(share, cols, n).transpose(2, 1, 0)
-    even_odd = bases[0].reshape(half, 2).T.astype(BF16)
-    sent = jnp.concatenate(
+    even_odd = bases[0].reshape(half, 2).T.astype(BF16).reshape(1, 2 * half)
+    second = jnp.concatenate(
         [
-            cot.reshape(n, cols * half),
-            jnp.broadcast_to(even_odd.reshape(1, 2 * half), (n, 2 * half)),
+            jnp.broadcast_to(even_odd, (n, 2 * half)),
             own.reshape(n, cols * share),
+            jnp.zeros((n, (cols - 2) * half - cols * share), BF16),
         ],
         axis=1,
     )
+    sent = jnp.stack([cot.reshape(n, cols * half), second], axis=1)
     got = exchange(sent)
-    cot = got[:, : cols * half].reshape(seq, win, cols, half).transpose(1, 2, 0, 3)
+    cot = got[:, 0].reshape(seq, win, cols, half).transpose(1, 2, 0, 3)
     cot = cot.reshape(win, cols, seq * half)
     dr = jnp.pad(0.5 * cot, ((0, 0), (0, 4 - cols), (0, 0)))
     dr = jnp.concatenate([dr, dr], axis=1)
-    sym = got[:, cols * half : (cols + 2) * half].reshape(seq, win, 2, half)
+    sym = got[:, 1, : 2 * half].reshape(seq, win, 2, half)
     sym = sym.transpose(1, 2, 0, 3).reshape(win, 2, seq * half).astype(F32)
-    weights = got[:, (cols + 2) * half :].reshape(n, cols, share)
+    weights = got[:, 1, 2 * half : 2 * half + cols * share].reshape(n, cols, share)
     weights = weights.transpose(1, 0, 2).reshape(cols, KW, channels).astype(F32)
 
     gained = stem_weight * norm_gain

time: 104 us -> 89.6 us (0.86)
  waiting for transfers between devices: 49.9 us -> 42 us
  Pallas kernels: 11.3 us -> 6.2 us
  local copies, waits for them, and re-layouts: 11.7 us -> 10.6 us
    all_to_all x3, waiting for transfers between devices: 49.9 us -> 42 us  [exchange(): return lax.all_to_all(x, AXES, 0, 0, tiled=True)]
    pallas_call x1, Pallas kernels: 11.3 us -> 6.2 us  [main_call(): pl.pallas_call(functools.partial(main_kernel, channels), out_shape=jax.Sh...]
    all_to_all x3 -> x1, local copies, waits for them, and re-layouts: 3.46 us -> 0.75 us  [exchange(): return lax.all_to_all(x, AXES, 0, 0, tiled=True)]
    another operation x0 -> x3, local copies, waits for them, and re-layouts: none -> 1.27 us  [the longest x2 1.24 us: shards(): sent = jnp.stack([cot.reshape(n, cols * half), second], axis=1)]
where the time goes in v2:
time: 89.6 us; the launch traced here: 89.2 us
  waiting for transfers between devices  42 us (47%)
  starting transfers between devices  27.3 us (30%)
  local copies, waits for them, and re-layouts  10.6 us (12%)
  Pallas kernels  6.2 us (7%)
  matrix products  1.1 us (1%)
  other arithmetic  1.07 us (1%)
  between operations  0.99 us (1%)
    all_to_all x3, waiting for transfers between devices, exchange(): return lax.all_to_all(x, AXES, 0, 0, tiled=True)  42 us
    all_to_all x3, starting transfers between devices, exchange(): return lax.all_to_all(x, AXES, 0, 0, tiled=True)  27.3 us
    pallas_call x1, Pallas kernels, main_call(): pl.pallas_call(functools.partial(main_kernel, channels), out_shape=jax.Sh...  6.2 us
    unnamed x11, local copies, waits for them, and re-layouts  1.93 us
  transfers between devices with their start and end apart: 3, of which 3 were waited for; matrix products, arithmetic and copies ran while one was open for 1% of the time, Pallas kernels for 0%

profile of v2, /device:TPU:1, one launch (start us, length us, event | category | flops | bytes accessed | tf_op | source)
XLA Modules:
  0.0 89.2 jit_solution(9376408530754396816)
XLA Ops:
  0.6 0.8 reshape.102
  1.6 0.5 copy-done.3
  2.1 0.2 convert_element_type.47
  2.5 0.1 copy.117
  2.7 0.8 copy-done.1
  3.4 0.2 copy.112
  3.6 0.2 copy.113
  3.8 1.1 %copy.118 = bf16[256,2,384]{2,1,0:T(2,128)(2,1)} copy(bf16[256,2,384]{0,2,1:T(8,128)(2,1)S(1)} %pad_maximum_fusion.1) | data formatting | bytes 786432 | tf_op jit(solution)/shard_map/stack | solution.py:132
  4.9 15.7 %all-to-all-start = ((bf16[256,2,384]{2,1,0:T(2,128)(2,1)}), bf16[256,2,384]{2,1,0:T(2,128)(2,1)S(1)}, u32[]{:S(2)}, u32[]{:S(2)}) async-start(bf16[256,2,384]{2,1,0:T(2,128)(2,1)} %copy.118), calls=%async_computation | async-start | bytes 786432 | tf_op jit(solution)/shard_map/all_to_all | solution.py:109
  20.7 0.2 convolution_multiply_fusion
  20.9 16.8 %all-to-all-done = bf16[256,2,384]{2,1,0:T(2,128)(2,1)S(1)} async-done(((bf16[256,2,384]{2,1,0:T(2,128)(2,1)}), bf16[256,2,384]{2,1,0:T(2,128)(2,1)S(1)}, u32[]{:S(2)}, u32[]{:S(2)}) %all-to-all-start) | async-done | bytes 393248 | tf_op jit(solution)/shard_map/all_to_all | solution.py:109
  38.0 0.2 copy.125
  38.2 0.3 reshape.104
  38.5 0.3 copy-done.2
  38.9 0.2 convolution_bitcast_fusion.2
  39.4 0.3 slice.82
  40.2 0.2 pad_maximum_fusion.dr_ref
  40.5 6.2 %shard_map.76 = f32[96,24]{1,0:T(8,128)S(1)} custom-call(f32[8,2,4096]{2,1,0:T(2,128)S(1)} %reshape.112.sym_ref, bf16[8,8,4096]{2,1,0:T(8,128)(2,1)S(1)} %pad_maximum_fusion.dr_ref, bf16[88,72]{1,0:T(8,128)(2,1)S(1)} %pad_maximum_fusion.3.table_ref), custom_call_target="tpu_custom_call" | custom-call | tf_op jit(solution)/shard_map/pallas_call | solution.py:99
  46.9 0.3 multiply_reduce_fusion
  47.1 0.2 convolution_bitcast_fusion.1
  47.4 0.3 convolution_subtract_fusion
  47.8 0.3 reshape.107
  48.1 0.2 copy.132
  48.3 0.7 copy.133
  49.1 6.2 %all-to-all-start.1 = ((f32[256,1,108]{2,1,0:T(1,128)}), f32[256,1,108]{2,1,0:T(1,128)S(1)}, u32[]{:S(2)}, u32[]{:S(2)}) async-start(f32[256,1,108]{2,1,0:T(1,128)} %copy.133), calls=%async_computation.1 | async-start | bytes 262144 | tf_op jit(solution)/shard_map/all_to_all | solution.py:109
  55.5 12.8 %all-to-all-done.1 = f32[256,1,108]{2,1,0:T(1,128)S(1)} async-done(((f32[256,1,108]{2,1,0:T(1,128)}), f32[256,1,108]{2,1,0:T(1,128)S(1)}, u32[]{:S(2)}, u32[]{:S(2)}) %all-to-all-start.1) | async-done | bytes 110624 | tf_op jit(solution)/shard_map/all_to_all | solution.py:109
  68.4 0.7 broadcast_in_dim.49
  69.1 5.4 %all-to-all-start.2 = ((f32[256,1,63]{2,1,0:T(1,128)}), f32[256,1,63]{2,1,0:T(1,128)S(1)}, u32[]{:S(2)}, u32[]{:S(2)}) async-start(f32[256,1,63]{2,1,0:T(1,128)} %broadcast_in_dim.49), calls=%async_computation.2 | async-start | bytes 262144 | tf_op jit(solution)/shard_map/all_to_all | solution.py:109
  74.7 0.6 reshape.110
  75.3 12.4 %all-to-all-done.2 = f32[256,1,63]{2,1,0:T(1,128)S(1)} async-done(((f32[256,1,63]{2,1,0:T(1,128)}), f32[256,1,63]{2,1,0:T(1,128)S(1)}, u32[]{:S(2)}, u32[]{:S(2)}) %all-to-all-start.2) | async-done | bytes 64544 | tf_op jit(solution)/shard_map/all_to_all | solution.py:109
  87.9 0.7 slice.80
  88.6 0.6 squeeze.5
  (55 shorter events, 2.7 us)
Async XLA Ops:
  1.4 0.7 copy-start.3
  2.5 0.9 %copy-start.1 = (bf16[1,128,768]{2,1,0:T(8,128)(2,1)S(1)}, bf16[1,128,768]{2,1,0:T(8,128)(2,1)}, u32[]{:S(2)}) copy-start(bf16[1,128,768]{2,1,0:T(8,128)(2,1)} %param.9) | copy-start | bytes 589828
  4.9 15.8 %copy-start = (f32[20,768]{1,0:T(8,128)S(1)}, f32[20,768]{1,0:T(8,128)}, u32[]{:S(2)}) copy-start(f32[20,768]{1,0:T(8,128)} %param.6) | copy-start | bytes 184324
  4.9 32.8 %all-to-all-start = ((bf16[256,2,384]{2,1,0:T(2,128)(2,1)}), bf16[256,2,384]{2,1,0:T(2,128)(2,1)S(1)}, u32[]{:S(2)}, u32[]{:S(2)}) async-start(bf16[256,2,384]{2,1,0:T(2,128)(2,1)} %copy.118), calls=%async_computation | async-start | bytes 786432 | tf_op jit(solution)/shard_map/all_to_all | solution.py:109
  38.2 0.7 copy-start.2
  49.1 19.2 %all-to-all-start.1 = ((f32[256,1,108]{2,1,0:T(1,128)}), f32[256,1,108]{2,1,0:T(1,128)S(1)}, u32[]{:S(2)}, u32[]{:S(2)}) async-start(f32[256,1,108]{2,1,0:T(1,128)} %copy.133), calls=%async_computation.1 | async-start | bytes 262144 | tf_op jit(solution)/shard_map/all_to_all | solution.py:109
  69.1 18.6 %all-to-all-start.2 = ((f32[256,1,63]{2,1,0:T(1,128)}), f32[256,1,63]{2,1,0:T(1,128)S(1)}, u32[]{:S(2)}, u32[]{:S(2)}) async-start(f32[256,1,63]{2,1,0:T(1,128)} %broadcast_in_dim.49), calls=%async_computation.2 | async-start | bytes 262144 | tf_op jit(solution)/shard_map/all_to_all | solution.py:109

commit v3 on v2

v3 whole, which is shorter than its diff:
```python
import functools

import jax
import jax.numpy as jnp
from jax import lax
from jax.experimental import pallas as pl
from jax.experimental.pallas import tpu as pltpu
from jax.sharding import PartitionSpec as P

KW = 5
TAPS = 4 * KW
AXES = ("seq", "win")
F32 = jnp.float32
BF16 = jnp.bfloat16
HIGH = lax.Precision.HIGHEST
ROOT = 0.7978845608028654
CUBE = 0.044715
ROWS, SUMS, LINE = 16, 24, 6
NN, NT = (((1,), (0,)), ((), ())), (((1,), (1,)), ((), ()))


def pieces(x, count):
    out = []
    for _ in range(count):
        top = x.astype(BF16)
        out.append(top)
        x = x - top.astype(F32)
    return out


def dot(a, b, dims, precision=None):
    return lax.dot_general(a, b, dims, precision=precision, preferred_element_type=F32)


def gelu_slope(x):
    sq = x * x
    th = jnp.tanh(ROOT * x * (1.0 + CUBE * sq))
    return 0.5 * (1.0 + th) + (0.5 * ROOT) * x * (1.0 - th * th) * (1.0 + 3.0 * CUBE * sq)


def pack_kernel(n, bases_ref, weight_ref, cot_ref, out_ref, hold):
    half = cot_ref.shape[0]
    share, channels = weight_ref.shape
    cols = channels // n
    for m in range(cols):
        hold[pl.ds(m, n, stride=LINE), :] = cot_ref[:, m * n : (m + 1) * n].astype(F32).T
    count = 2 * half
    place = lax.broadcasted_iota(jnp.int32, (count, count), 0)
    lane = lax.broadcasted_iota(jnp.int32, (count, count), 1)
    wanted = jnp.where(lane < half, 2 * lane, 2 * (lane - half) + 1)
    pick = (place == wanted).astype(BF16)
    row = bases_ref[...].astype(F32).astype(BF16)
    split = dot(jnp.broadcast_to(row, (8, count)), pick, NN)
    hold[pl.ds(3, n, stride=LINE), :] = jnp.broadcast_to(split[0:1, :half], (n, half))
    hold[pl.ds(4, n, stride=LINE), :] = jnp.broadcast_to(split[0:1, half:], (n, half))
    weight = weight_ref[...].astype(F32)
    rows = []
    for m in range(cols):
        rows += [weight[:, m * n : (m + 1) * n], jnp.zeros((ROWS - share, n), F32)]
    rows.append(jnp.zeros((half - cols * ROWS, n), F32))
    hold[pl.ds(5, n, stride=LINE), :] = jnp.concatenate(rows, axis=0).T
    out_ref[...] = hold[...].astype(BF16)


def main_kernel(
    seq, win, me_ref, got_ref, stem_ref, gain_ref, gained_ref, gram_ref, chosen_ref, turn_ref, out_ref, hold
):
    n = seq * win
    channels = stem_ref.shape[1]
    cols = channels // n
    lanes = seq * 128
    hold[: LINE * n, :] = got_ref[...].astype(F32)
    hold[LINE * n :, :] = jnp.zeros((8, 128), F32)
    chosen = chosen_ref[...]
    turn = turn_ref[...]

    own = hold[pl.ds(5, n, stride=LINE), :].T[: ROWS * cols]
    spread = dot(own.astype(BF16), chosen, NN)
    line = [
        jnp.sum(spread[ROWS * m : ROWS * (m + 1)] * turn, axis=0, keepdims=True)
        for m in range(cols)
    ]
    line = jnp.concatenate(line + [jnp.zeros_like(line[0])] * (4 - cols), axis=0)
    weights = jnp.concatenate(
        [line[:, t * channels : (t + 1) * channels] for t in range(KW)], axis=0
    ).astype(BF16)
    mixed = dot(weights, gained_ref[...], NT)
    mixed = mixed[:, 0:TAPS] + mixed[:, 24 : 24 + TAPS] + mixed[:, 48 : 48 + TAPS]
    blank = jnp.zeros((4, 4), F32)
    table = []
    for t in range(KW):
        tap = mixed[4 * t : 4 * t + 4]
        pair = [jnp.concatenate([tap, blank], axis=1), jnp.concatenate([blank, tap], axis=1)]
        table += pair if t % 2 == 0 else pair[::-1]
    table = [part.astype(F32) for part in pieces(jnp.concatenate(table, axis=0), 3)]
    table = jnp.concatenate([jnp.concatenate(table, axis=1), gram_ref[...]], axis=0).astype(BF16)

    sub = lax.broadcasted_iota(jnp.int32, (8, 128), 0)
    lane = lax.broadcasted_iota(jnp.int32, (8, lanes), 1)
    wide = lax.broadcasted_iota(jnp.int32, (8, lanes), 0)
    top = wide < 4
    first, last = lane == 0, lane == lanes - 1
    base = (wide % 4).astype(F32)

    def down(x, fill):
        return jnp.where(first, fill, pltpu.roll(x, 1, 1))

    def up(x, fill):
        return jnp.where(last, fill, pltpu.roll(x, lanes - 1, 1))

    total = jnp.zeros((96, 24), F32)
    for w in range(win):
        dr, mid = [], []
        for s in range(seq):
            at = LINE * (s * win + w)
            cell = jnp.where(sub < cols, 0.5 * hold[at : at + 8, :], 0.0)
            dr.append(cell + pltpu.roll(cell, 4, 0))
            mid.append(
                jnp.where(
                    sub < 4,
                    jnp.broadcast_to(hold[at + 3 : at + 4, :], (8, 128)),
                    jnp.broadcast_to(hold[at + 4 : at + 5, :], (8, 128)),
                )
            )
        dr, mid = jnp.concatenate(dr, axis=1), jnp.concatenate(mid, axis=1)
        hots = jnp.concatenate(
            [(cell == base).astype(F32) for cell in (down(mid, -1.0), mid, up(mid, -1.0))], axis=0
        )
        narrow = hots.astype(BF16)
        looked = dot(table, jnp.concatenate([narrow] * 3, axis=0), NN)
        taps = [looked[8 * t : 8 * t + 8] for t in range(KW)]
        mean_e = jnp.sum(looked[40:64] * hots, axis=0, keepdims=True)
        mean_o = jnp.sum(looked[64:88] * hots, axis=0, keepdims=True)
        scale_e = lax.rsqrt(mean_e + 1e-06)
        scale_o = lax.rsqrt(mean_o + 1e-06)
        scale = jnp.where(top, scale_e, scale_o)
        swapped = jnp.where(top, scale_o, scale_e)
        p0, p2, p4 = taps[0] * scale, taps[2] * scale, taps[4] * scale
        p1, p3 = taps[1] * swapped, taps[3] * swapped
        pre = down(p0 + jnp.where(top, p1, 0.0), 0.0)
        pre = pre + p2 + jnp.where(top, p3, p1)
        pre = pre + up(p4 + jnp.where(top, 0.0, p3), 0.0)
        dpre = dr * gelu_slope(pre)
        ahead, behind = up(dpre, 0.0), down(dpre, 0.0)
        d1 = jnp.where(top, ahead, dpre)
        d3 = jnp.where(top, dpre, behind)
        here = taps[0] * ahead + taps[2] * dpre + taps[4] * behind
        there = taps[1] * d1 + taps[3] * d3
        both = here + pltpu.roll(there, 4, 0)
        q_e = jnp.sum(jnp.where(top, both, 0.0), axis=0, keepdims=True)
        q_o = jnp.sum(jnp.where(top, 0.0, both), axis=0, keepdims=True)
        u_e = q_e * scale_e * scale_e * scale_e * (1.0 / channels)
        u_o = q_o * scale_o * scale_o * scale_o * (1.0 / channels)
        rows = [ahead * scale, d1 * swapped, dpre * scale, d3 * swapped, behind * scale, dr]
        rows = jnp.concatenate(rows + [hots * u_e, hots * u_o], axis=0)
        total = total + dot(rows.astype(BF16), narrow, NT)

    stem = stem_ref[...]
    gain = gain_ref[...]
    sums = []
    for t in range(KW + 1):
        cell = total[8 * t : 8 * t + 8]
        even, odd = (cell[0:4], cell[4:8]) if t % 2 == 0 or t == KW else (cell[4:8], cell[0:4])
        sums.append(even[:, :TAPS] + odd[:, 4:])
    grads = jnp.concatenate(sums[:KW], axis=0)
    crossed = total[48 : 48 + TAPS, :TAPS] + total[76:96, 4:]
    conv = dot(grads, stem * gain, NN, HIGH)
    conv = jnp.concatenate([conv[4 * t : 4 * t + 4] for t in range(KW)], axis=1)
    conv = jnp.concatenate([conv[m : m + 1] * turn for m in range(cols)], axis=0)
    conv = pieces(conv, 2)
    conv = dot(conv[0], chosen, NT) + dot(conv[1], chosen, NT)
    back = jnp.zeros((TAPS, channels), F32)
    for part in pieces(grads.T, 3):
        back = back + dot(part, weights, NN)
    stem_part = gain * back - dot(crossed, stem, NN, HIGH)
    gain_part = jnp.sum(stem * back, axis=0, keepdims=True)
    small = jnp.concatenate([stem_part, gain_part, jnp.zeros((3, channels), F32)], axis=0)
    direct = jnp.concatenate([sums[KW].T, jnp.zeros((4, 4), F32)], axis=0)
    mine = lax.broadcasted_iota(jnp.int32, (SUMS, n), 1) == me_ref[0]
    rows = [conv]
    for m in range(cols):
        rows.append(small[:, m * n : (m + 1) * n] + jnp.where(mine, direct[:, m : m + 1], 0.0))
    rows.append(jnp.zeros((128 - cols * (ROWS + SUMS), n), F32))
    out_ref[...] = jnp.concatenate(rows, axis=0).T


def finish_kernel(got_ref, stem_ref, gain_ref):
    n = got_ref.shape[0]
    turned = got_ref[...].T
    for m in range(stem_ref.shape[1] // n):
        stem_ref[:, m * n : (m + 1) * n] = turned[SUMS * m : SUMS * m + TAPS]
        gain_ref[:, m * n : (m + 1) * n] = turned[SUMS * m + TAPS : SUMS * m + TAPS + 1]


def call(kernel, name, out, operands, scratch=(), smem=0):
    space = [pl.BlockSpec(memory_space=pltpu.SMEM)] * smem
    space += [pl.BlockSpec(memory_space=pltpu.VMEM)] * (len(operands) - smem)
    many = isinstance(out, tuple)
    spec = pl.BlockSpec(memory_space=pltpu.VMEM)
    return pl.pallas_call(
        kernel,
        name=name,
        out_shape=out,
        in_specs=space,
        out_specs=(spec,) * len(out) if many else spec,
        scratch_shapes=list(scratch),
        compiler_params=pltpu.CompilerParams(vmem_limit_bytes=48 * 1024 * 1024),
    )(*operands)


def exchange(x):
    return lax.all_to_all(x, AXES, 0, 0, tiled=True)


def shards(bases, stem_weight, norm_gain, conv_weight, cotangent):
    seq, win = lax.axis_size("seq"), lax.axis_size("win")
    n = seq * win
    channels = norm_gain.shape[0]
    cols = channels // n
    half = bases.shape[1] // 2
    share = conv_weight.shape[0]
    me = lax.axis_index("seq") * win + lax.axis_index("win")

    sent = call(
        functools.partial(pack_kernel, n),
        "pack",
        jax.ShapeDtypeStruct((LINE * n, half), BF16),
        (bases, conv_weight, cotangent[0]),
        [pltpu.VMEM((LINE * n, half), F32)],
    )
    got = exchange(sent.reshape(n, LINE // 2, 2, half)).reshape(LINE * n, half)

    gained = stem_weight * norm_gain
    gained = [jnp.pad(part, ((0, 4), (0, 0))) for part in pieces(gained, 3)]
    gained = jnp.concatenate(gained, axis=0)
    gram = jnp.dot(stem_weight, stem_weight.T, precision=HIGH) * (1.0 / channels)
    gram = jnp.concatenate(
        [jnp.pad(gram, ((0, 4), (0, 4))), jnp.pad(gram, ((4, 0), (4, 0)))], axis=0
    )
    gram = jnp.concatenate([part.astype(F32) for part in pieces(gram, 3)], axis=1)
    row = jnp.arange(KW * channels, dtype=jnp.int32)[None, :]
    chosen = (row // share == jnp.arange(n, dtype=jnp.int32)[:, None]).astype(BF16)
    turn = (row % share == jnp.arange(ROWS, dtype=jnp.int32)[:, None]).astype(F32)

    packed = call(
        functools.partial(main_kernel, seq, win),
        "main",
        jax.ShapeDtypeStruct((n, 128), F32),
        (me.reshape(1), got, stem_weight, norm_gain[None], gained, gram, chosen, turn),
        [pltpu.VMEM((LINE * n + 8, 128), F32)],
        1,
    )
    got = exchange(packed)
    conv_grad = jnp.concatenate(
        [got[:, ROWS * m : ROWS * m + share].T for m in range(cols)], axis=1
    )
    mine = jnp.sum(got[:, cols * ROWS : cols * (ROWS + SUMS)], axis=0, keepdims=True)
    full = exchange(jnp.broadcast_to(mine, (n, mine.shape[1])))
    stem_grad, gain_grad = call(
        finish_kernel,
        "finish",
        (
            jax.ShapeDtypeStruct((TAPS, channels), F32),
            jax.ShapeDtypeStruct((1, channels), F32),
        ),
        (full,),
    )
    return (conv_grad, stem_grad, gain_grad[0])


def solution(mesh):
    in_specs = (P("win", "seq"), P(), P(), P(("seq", "win"), None), P("win", "seq", None))
    out_specs = (P(("seq", "win"), None), P(), P())
    return jax.shard_map(shards, mesh=mesh, in_specs=in_specs, out_specs=out_specs, check_vma=False)
```

time: 89.6 us -> 86.3 us (0.963)
  blocking collectives: 0 us -> 19 us
  waiting for transfers between devices: 42 us -> 25.8 us
  local copies, waits for them, and re-layouts: 10.6 us -> 4.14 us
  starting transfers between devices: 27.3 us -> 21.2 us
  Pallas kernels: 6.2 us -> 10.9 us
  other arithmetic: 1.07 us -> 2.9 us
    all_to_all x0 -> x1, blocking collectives: none -> 19 us  [exchange(): return lax.all_to_all(x, AXES, 0, 0, tiled=True)]
    all_to_all x3 -> x2, waiting for transfers between devices: 42 us -> 25.8 us  [exchange(): return lax.all_to_all(x, AXES, 0, 0, tiled=True)]
    all_to_all x3 -> x2, starting transfers between devices: 27.3 us -> 21.2 us  [exchange(): return lax.all_to_all(x, AXES, 0, 0, tiled=True)]
    pallas_call x1 -> x3, Pallas kernels: 6.2 us -> 10.9 us  [call(): pl.pallas_call(kernel, name=name, out_shape=out, in_specs=space, out_spec...]
    reshape x9 -> x0, local copies, waits for them, and re-layouts: 2.35 us -> none  [the longest x1 0.76 us: shards(): own = conv_weight.reshape(share, cols, n).transpose(2, 1, 0)]
    slice x10 -> x0, local copies, waits for them, and re-layouts: 1.53 us -> none  [the longest x4 0.92 us: shards(): return (conv_grad, full[:taps], full[taps])]
    another operation x3 -> x0, local copies, waits for them, and re-layouts: 1.27 us -> none  [the longest x2 1.24 us: shards(): sent = jnp.stack([cot.reshape(n, cols * half), second], axis=1)]
    dot_general x1, matrix products: 0.18 us -> 1.16 us  [shards(): jnp.dot(stem_weight, stem_weight.T, precision=HIGH) * (1.0 / channels)]
  transfers between devices with their start and end apart: 3 -> 2, of which waited for: 3 -> 2; matrix products, arithmetic and copies ran while one was open for 1% -> 5% of each run, Pallas kernels for 0% -> 0%
where the time goes in v3:
time: 86.3 us; the launch traced here: 85.8 us
  waiting for transfers between devices  25.8 us (30%)
  starting transfers between devices  21.2 us (25%)
  blocking collectives  19 us (22%)
  Pallas kernels  10.9 us (13%)
  local copies, waits for them, and re-layouts  4.14 us (5%)
  other arithmetic  2.9 us (3%)
  matrix products  1.16 us (1%)
    all_to_all x2, waiting for transfers between devices, exchange(): return lax.all_to_all(x, AXES, 0, 0, tiled=True)  25.8 us
    all_to_all x2, starting transfers between devices, exchange(): return lax.all_to_all(x, AXES, 0, 0, tiled=True)  21.2 us
    all_to_all x1, blocking collectives, exchange(): return lax.all_to_all(x, AXES, 0, 0, tiled=True)  19 us
    pallas_call x3, Pallas kernels, call(): pl.pallas_call(kernel, name=name, out_shape=out, in_specs=space, out_spec...  10.9 us
    unnamed x8, local copies, waits for them, and re-layouts  2.34 us
  transfers between devices with their start and end apart: 2, of which 2 were waited for; matrix products, arithmetic and copies ran while one was open for 5% of the time, Pallas kernels for 0%

profile of v3, /device:TPU:1, one launch (start us, length us, event | category | flops | bytes accessed | tf_op | source)
XLA Modules:
  0.0 85.8 jit_solution(4174765380380558284)
XLA Ops:
  0.6 0.0 copy-start.1
  0.6 0.9 %copy-done.1 = bf16[1,128,768]{2,1,0:T(8,128)(2,1)S(1)} copy-done((bf16[1,128,768]{2,1,0:T(8,128)(2,1)S(1)}, bf16[1,128,768]{2,1,0:T(8,128)(2,1)}, u32[]{:S(2)}) %copy-start.1) | copy-done | bytes 196632
  1.6 0.0 copy-start.2
  1.6 0.7 copy-done.2
  2.3 0.0 copy-start.3
  2.3 0.7 copy-done.3
  3.0 1.0 %pack.1 = bf16[1536,128]{1,0:T(8,128)(2,1)} custom-call(s32[1,256]{1,0:T(1,128)S(1)} %copy-done.3, bf16[15,768]{1,0:T(8,128)(2,1)S(1)} %copy-done.2, bf16[128,768]{1,0:T(8,128)(2,1)S(1)} %bitcast.20), custom_call_target="tpu_custom_call" | custom-call | tf_op jit(solution)/shard_map/pack/pallas_call | solution.py:200
  3.9 0.0 copy-start
  3.9 15.7 %all-to-all-start = ((bf16[256,3,2,128]{3,2,1,0:T(2,128)(2,1)}), bf16[256,3,2,128]{3,2,1,0:T(2,128)(2,1)S(1)}, u32[]{:S(2)}, u32[]{:S(2)}) async-start(bf16[256,3,2,128]{3,2,1,0:T(2,128)(2,1)} %bitcast.2), calls=%async_computation | async-start | bytes 786432 | tf_op jit(solution)/shard_map/all_to_all | solution.py:212
  19.6 1.2 %convolution_multiply_fusion = f32[20,20]{1,0:T(8,128)S(1)} fusion(f32[20,768]{1,0:T(8,128)} %stem_ref.1), kind=kOutput, calls=%fused_computation.2 | convolution fusion | flops 3686800 | bytes 63040 | tf_op jit(solution)/shard_map/dot_general | solution.py:236
  20.8 0.1 fusion.18
  20.9 0.1 convert_convert_fusion
  21.0 0.7 broadcast_in_dim.4.gain_ref
  21.7 0.9 %multiply_convert_fusion = (bf16[20,768]{1,0:T(8,128)(2,1)S(1)}, bf16[20,768]{1,0:T(8,128)(2,1)S(1)}, bf16[20,768]{1,0:T(8,128)(2,1)S(1)}) fusion(f32[20,768]{1,0:T(8,128)} %stem_ref.1, f32[768]{0:T(1024)} %param.7), kind=kLoop, calls=%fused_computation.21 | loop fusion | flops 122880 | bytes 156672 | tf_op jit(solution)/shard_map/convert_element_type | solution.py:25
  22.6 0.3 fusion.chosen_ref
  22.9 0.1 pad_maximum_fusion.1.gram_ref
  23.1 13.7 %all-to-all-done = bf16[256,3,2,128]{3,2,1,0:T(2,128)(2,1)S(1)} async-done(((bf16[256,3,2,128]{3,2,1,0:T(2,128)(2,1)}), bf16[256,3,2,128]{3,2,1,0:T(2,128)(2,1)S(1)}, u32[]{:S(2)}, u32[]{:S(2)}) %all-to-all-start) | async-done | bytes 393248 | tf_op jit(solution)/shard_map/all_to_all | solution.py:212
  36.8 0.0 copy-done
  36.8 9.2 %main.1 = f32[256,128]{1,0:T(8,128)S(1)} custom-call(s32[1]{0:T(128)} %bitcast.me_ref, bf16[1536,128]{1,0:T(8,128)(2,1)S(1)} %bitcast.17, f32[20,768]{1,0:T(8,128)S(1)} %copy-done, f32[1,768]{1,0:T(1,128)S(1)} %broadcast_in_dim.4.gain_ref, bf16[72,768]{1,0:T(8,128)(2,1)S(1)} %fusion.7.gained_ref, f32[48,72]{1,0:T(8,128)S(1)} %pad_maximum_fusion.1.gram_ref, ...), custom_call_target="tpu_custom_call" | custom-call | tf_op jit(solution)/shard_map/main/pallas_call | solution.py:200
  46.0 19.0 %all_to_all.25 = f32[256,1,128]{2,1,0:T(1,128)S(1)} all-to-all(f32[256,1,128]{2,1,0:T(1,128)S(1)} %bitcast.19), channel_id=1, replica_groups=mesh['seq'=32,'win'=8] {'seq','win'}, dimensions={0} | all-to-all | bytes 262144 | tf_op jit(solution)/shard_map/all_to_all | solution.py:212
  65.0 0.1 slice_reduce_fusion
  65.1 0.7 broadcast_in_dim.5
  65.8 5.5 %all-to-all-start.2 = ((f32[256,1,72]{2,1,0:T(1,128)}), f32[256,1,72]{2,1,0:T(1,128)S(1)}, u32[]{:S(2)}, u32[]{:S(2)}) async-start(f32[256,1,72]{2,1,0:T(1,128)} %broadcast_in_dim.5), calls=%async_computation.2 | async-start | bytes 262144 | tf_op jit(solution)/shard_map/all_to_all | solution.py:212
  71.4 0.1 slice_bitcast_fusion.2
  71.5 0.1 copy.17
  71.6 0.1 copy.19
  71.7 0.1 copy.18
  71.8 0.6 pad_maximum_fusion
  72.4 12.1 %all-to-all-done.2 = f32[256,1,72]{2,1,0:T(1,128)S(1)} async-done(((f32[256,1,72]{2,1,0:T(1,128)}), f32[256,1,72]{2,1,0:T(1,128)S(1)}, u32[]{:S(2)}, u32[]{:S(2)}) %all-to-all-start.2) | async-done | bytes 73760 | tf_op jit(solution)/shard_map/all_to_all | solution.py:212
  84.5 0.7 finish.1
  85.2 0.6 reduce
  (4 shorter events, 0.1 us)
Async XLA Ops:
  0.6 0.9 %copy-start.1 = (bf16[1,128,768]{2,1,0:T(8,128)(2,1)S(1)}, bf16[1,128,768]{2,1,0:T(8,128)(2,1)}, u32[]{:S(2)}) copy-start(bf16[1,128,768]{2,1,0:T(8,128)(2,1)} %param.9) | copy-start | bytes 589828
  1.6 0.7 copy-start.2
  2.3 0.7 copy-start.3
  3.9 32.8 %copy-start = (f32[20,768]{1,0:T(8,128)S(1)}, f32[20,768]{1,0:T(8,128)}, u32[]{:S(2)}) copy-start(f32[20,768]{1,0:T(8,128)} %stem_ref.1) | copy-start | bytes 184324
  3.9 32.8 %all-to-all-start = ((bf16[256,3,2,128]{3,2,1,0:T(2,128)(2,1)}), bf16[256,3,2,128]{3,2,1,0:T(2,128)(2,1)S(1)}, u32[]{:S(2)}, u32[]{:S(2)}) async-start(bf16[256,3,2,128]{3,2,1,0:T(2,128)(2,1)} %bitcast.2), calls=%async_computation | async-start | bytes 786432 | tf_op jit(solution)/shard_map/all_to_all | solution.py:212
  65.8 18.7 %all-to-all-start.2 = ((f32[256,1,72]{2,1,0:T(1,128)}), f32[256,1,72]{2,1,0:T(1,128)S(1)}, u32[]{:S(2)}, u32[]{:S(2)}) async-start(f32[256,1,72]{2,1,0:T(1,128)} %broadcast_in_dim.5), calls=%async_computation.2 | async-start | bytes 262144 | tf_op jit(solution)/shard_map/all_to_all | solution.py:212

commit v4 on v3

--- a/solution.py
+++ b/solution.py
@@ -16,6 +16,7 @@
 ROOT = 0.7978845608028654
 CUBE = 0.044715
 ROWS, SUMS, LINE = 16, 24, 6
+CELLS = 4
 NN, NT = (((1,), (0,)), ((), ())), (((1,), (1,)), ((), ()))
 
 
@@ -38,7 +39,17 @@
     return 0.5 * (1.0 + th) + (0.5 * ROOT) * x * (1.0 - th * th) * (1.0 + 3.0 * CUBE * sq)
 
 
-def pack_kernel(n, bases_ref, weight_ref, cot_ref, out_ref, hold):
+def pack_kernel(n, bases_hbm, weight_hbm, cot_hbm, out_ref, bases_ref, weight_ref, cot_ref, hold, sems):
+    copies = [
+        pltpu.make_async_copy(*pair, sems.at[i])
+        for i, pair in enumerate(
+            ((cot_hbm, cot_ref), (weight_hbm, weight_ref), (bases_hbm, bases_ref))
+        )
+    ]
+    for copy in copies:
+        copy.start()
+    for copy in copies:
+        copy.wait()
     half = cot_ref.shape[0]
     share, channels = weight_ref.shape
     cols = channels // n
@@ -68,7 +79,6 @@
     n = seq * win
     channels = stem_ref.shape[1]
     cols = channels // n
-    lanes = seq * 128
     hold[: LINE * n, :] = got_ref[...].astype(F32)
     hold[LINE * n :, :] = jnp.zeros((8, 128), F32)
     chosen = chosen_ref[...]
@@ -93,25 +103,27 @@
         pair = [jnp.concatenate([tap, blank], axis=1), jnp.concatenate([blank, tap], axis=1)]
         table += pair if t % 2 == 0 else pair[::-1]
     table = [part.astype(F32) for part in pieces(jnp.concatenate(table, axis=0), 3)]
-    table = jnp.concatenate([jnp.concatenate(table, axis=1), gram_ref[...]], axis=0).astype(BF16)
-
+    table = jnp.concatenate([jnp.concatenate(table, axis=1), jnp.zeros((32, 72), F32)], axis=0)
+    table = (table + gram_ref[...]).astype(BF16)
+
+    width = 128 * CELLS
+    count = seq // CELLS
     sub = lax.broadcasted_iota(jnp.int32, (8, 128), 0)
-    lane = lax.broadcasted_iota(jnp.int32, (8, lanes), 1)
-    wide = lax.broadcasted_iota(jnp.int32, (8, lanes), 0)
+    lane = lax.broadcasted_iota(jnp.int32, (8, width), 1)
+    wide = lax.broadcasted_iota(jnp.int32, (8, width), 0)
     top = wide < 4
-    first, last = lane == 0, lane == lanes - 1
+    first, last = lane == 0, lane == width - 1
     base = (wide % 4).astype(F32)
 
-    def down(x, fill):
-        return jnp.where(first, fill, pltpu.roll(x, 1, 1))
-
-    def up(x, fill):
-        return jnp.where(last, fill, pltpu.roll(x, lanes - 1, 1))
-
-    total = jnp.zeros((96, 24), F32)
-    for w in range(win):
+    def ahead_of(x):
+        return pltpu.roll(x, width - 1, 1)
+
+    def behind_of(x):
+        return pltpu.roll(x, 1, 1)
+
+    def load(w, c):
         dr, mid = [], []
-        for s in range(seq):
+        for s in range(c * CELLS, (c + 1) * CELLS):
             at = LINE * (s * win + w)
             cell = jnp.where(sub < cols, 0.5 * hold[at : at + 8, :], 0.0)
             dr.append(cell + pltpu.roll(cell, 4, 0))
@@ -122,26 +134,42 @@
                     jnp.broadcast_to(hold[at + 4 : at + 5, :], (8, 128)),
                 )
             )
-        dr, mid = jnp.concatenate(dr, axis=1), jnp.concatenate(mid, axis=1)
-        hots = jnp.concatenate(
-            [(cell == base).astype(F32) for cell in (down(mid, -1.0), mid, up(mid, -1.0))], axis=0
-        )
+        mid = jnp.concatenate(mid, axis=1)
+        return jnp.concatenate(dr, axis=1), mid, ahead_of(mid), behind_of(mid)
+
+    def look(prior, cell, later):
+        dr, mid, left, right = cell
+        down = jnp.where(first, -1.0 if prior is None else prior[3], right)
+        up = jnp.where(last, -1.0 if later is None else later[2], left)
+        hots = jnp.concatenate([(x == base).astype(F32) for x in (down, mid, up)], axis=0)
         narrow = hots.astype(BF16)
         looked = dot(table, jnp.concatenate([narrow] * 3, axis=0), NN)
         taps = [looked[8 * t : 8 * t + 8] for t in range(KW)]
-        mean_e = jnp.sum(looked[40:64] * hots, axis=0, keepdims=True)
-        mean_o = jnp.sum(looked[64:88] * hots, axis=0, keepdims=True)
+        mean_e = jnp.sum(looked[40:56] * hots[0:16], axis=0, keepdims=True) + looked[3:4]
+        mean_o = jnp.sum(looked[56:72] * hots[8:24], axis=0, keepdims=True) + looked[7:8]
         scale_e = lax.rsqrt(mean_e + 1e-06)
         scale_o = lax.rsqrt(mean_o + 1e-06)
         scale = jnp.where(top, scale_e, scale_o)
         swapped = jnp.where(top, scale_o, scale_e)
         p0, p2, p4 = taps[0] * scale, taps[2] * scale, taps[4] * scale
         p1, p3 = taps[1] * swapped, taps[3] * swapped
-        pre = down(p0 + jnp.where(top, p1, 0.0), 0.0)
-        pre = pre + p2 + jnp.where(top, p3, p1)
-        pre = pre + up(p4 + jnp.where(top, 0.0, p3), 0.0)
+        down = behind_of(p0 + jnp.where(top, p1, 0.0))
+        up = ahead_of(p4 + jnp.where(top, 0.0, p3))
+        return (p2 + jnp.where(top, p3, p1), up, down), (
+            hots, narrow, taps, scale_e, scale_o, scale, swapped, dr
+        )
+
+    def slope(prior, cell, later, dr):
+        pre = cell[0] + jnp.where(first, 0.0 if prior is None else prior[2], cell[2])
+        pre = pre + jnp.where(last, 0.0 if later is None else later[1], cell[1])
         dpre = dr * gelu_slope(pre)
-        ahead, behind = up(dpre, 0.0), down(dpre, 0.0)
+        return dpre, ahead_of(dpre), behind_of(dpre)
+
+    def close(prior, cell, later, kept):
+        hots, narrow, taps, scale_e, scale_o, scale, swapped, dr = kept
+        dpre = cell[0]
+        ahead = jnp.where(last, 0.0 if later is None else later[1], cell[1])
+        behind = jnp.where(first, 0.0 if prior is None else prior[2], cell[2])
         d1 = jnp.where(top, ahead, dpre)
         d3 = jnp.where(top, dpre, behind)
         here = taps[0] * ahead + taps[2] * dpre + taps[4] * behind
@@ -151,9 +179,31 @@
         q_o = jnp.sum(jnp.where(top, 0.0, both), axis=0, keepdims=True)
         u_e = q_e * scale_e * scale_e * scale_e * (1.0 / channels)
         u_o = q_o * scale_o * scale_o * scale_o * (1.0 / channels)
-        rows = [ahead * scale, d1 * swapped, dpre * scale, d3 * swapped, behind * scale, dr]
-        rows = jnp.concatenate(rows + [hots * u_e, hots * u_o], axis=0)
-        total = total + dot(rows.astype(BF16), narrow, NT)
+        lead = jnp.where(wide == 3, u_e, jnp.where(wide == 7, u_o, ahead * scale))
+        rows = [lead, d1 * swapped, dpre * scale, d3 * swapped, behind * scale, dr]
+        rows = jnp.concatenate(rows, axis=0).astype(BF16)
+        u_e, u_o = u_e.astype(BF16) * narrow[0:16], u_o.astype(BF16) * hots[8:24].astype(BF16)
+        return dot(jnp.concatenate([rows, u_e, u_o], axis=0), narrow, NT)
+
+    def at(items, i):
+        return items[i] if 0 <= i < len(items) else None
+
+    total = jnp.zeros((80, 24), F32)
+    for w in range(win):
+        loaded, looked, kept, slopes = [load(w, 0)], [], [], []
+        for step in range(count + 2):
+            if step + 1 < count:
+                loaded.append(load(w, step + 1))
+            if step < count:
+                part, keep = look(at(loaded, step - 1), loaded[step], at(loaded, step + 1))
+                looked.append(part)
+                kept.append(keep)
+            if 0 <= step - 1 < count:
+                c = step - 1
+                slopes.append(slope(at(looked, c - 1), looked[c], at(looked, c + 1), kept[c][7]))
+            if 0 <= step - 2 < count:
+                c = step - 2
+                total = total + close(at(slopes, c - 1), slopes[c], at(slopes, c + 1), kept[c])
 
     stem = stem_ref[...]
     gain = gain_ref[...]
@@ -163,12 +213,17 @@
         even, odd = (cell[0:4], cell[4:8]) if t % 2 == 0 or t == KW else (cell[4:8], cell[0:4])
         sums.append(even[:, :TAPS] + odd[:, 4:])
     grads = jnp.concatenate(sums[:KW], axis=0)
-    crossed = total[48 : 48 + TAPS, :TAPS] + total[76:96, 4:]
+    even, odd = total[48:64, :TAPS], total[64:80, 4:]
+    same = lax.broadcasted_iota(jnp.int32, (4, 4), 0) == lax.broadcasted_iota(jnp.int32, (4, 4), 1)
+    even_end = [even[:, 16:].T, jnp.where(same, total[3:4, 16:TAPS], 0.0)]
+    odd_end = [jnp.where(same, total[7:8, 4:8], 0.0), odd[:, :4].T]
+    crossed = jnp.concatenate([even, jnp.concatenate(even_end, axis=1)], axis=0)
+    crossed = crossed + jnp.concatenate([jnp.concatenate(odd_end, axis=1), odd], axis=0)
     conv = dot(grads, stem * gain, NN, HIGH)
     conv = jnp.concatenate([conv[4 * t : 4 * t + 4] for t in range(KW)], axis=1)
     conv = jnp.concatenate([conv[m : m + 1] * turn for m in range(cols)], axis=0)
-    conv = pieces(conv, 2)
-    conv = dot(conv[0], chosen, NT) + dot(conv[1], chosen, NT)
+    conv = dot(jnp.concatenate(pieces(conv, 2), axis=0), chosen, NT)
+    conv = conv[: ROWS * cols] + conv[ROWS * cols :]
     back = jnp.zeros((TAPS, channels), F32)
     for part in pieces(grads.T, 3):
         back = back + dot(part, weights, NN)
@@ -184,27 +239,33 @@
     out_ref[...] = jnp.concatenate(rows, axis=0).T
 
 
+def reduce_kernel(got_ref, out_ref):
+    out_ref[...] = jnp.broadcast_to(jnp.sum(got_ref[...], axis=0, keepdims=True), out_ref.shape)
+
+
 def finish_kernel(got_ref, stem_ref, gain_ref):
     n = got_ref.shape[0]
+    cols = stem_ref.shape[1] // n
     turned = got_ref[...].T
-    for m in range(stem_ref.shape[1] // n):
-        stem_ref[:, m * n : (m + 1) * n] = turned[SUMS * m : SUMS * m + TAPS]
-        gain_ref[:, m * n : (m + 1) * n] = turned[SUMS * m + TAPS : SUMS * m + TAPS + 1]
-
-
-def call(kernel, name, out, operands, scratch=(), smem=0):
-    space = [pl.BlockSpec(memory_space=pltpu.SMEM)] * smem
-    space += [pl.BlockSpec(memory_space=pltpu.VMEM)] * (len(operands) - smem)
+    for m in range(cols):
+        at = ROWS * cols + SUMS * m
+        stem_ref[:, m * n : (m + 1) * n] = turned[at : at + TAPS]
+        gain_ref[m * n : (m + 1) * n] = turned[at + TAPS]
+
+
+def call(kernel, name, out, operands, scratch=(), smem=0, space=pltpu.VMEM, limit=48):
+    specs = [pl.BlockSpec(memory_space=pltpu.SMEM)] * smem
+    specs += [pl.BlockSpec(memory_space=space)] * (len(operands) - smem)
     many = isinstance(out, tuple)
     spec = pl.BlockSpec(memory_space=pltpu.VMEM)
     return pl.pallas_call(
         kernel,
         name=name,
         out_shape=out,
-        in_specs=space,
+        in_specs=specs,
         out_specs=(spec,) * len(out) if many else spec,
         scratch_shapes=list(scratch),
-        compiler_params=pltpu.CompilerParams(vmem_limit_bytes=48 * 1024 * 1024),
+        compiler_params=pltpu.CompilerParams(vmem_limit_bytes=limit * 1024 * 1024),
     )(*operands)
 
 
@@ -226,7 +287,15 @@
         "pack",
         jax.ShapeDtypeStruct((LINE * n, half), BF16),
         (bases, conv_weight, cotangent[0]),
-        [pltpu.VMEM((LINE * n, half), F32)],
+        [
+            pltpu.VMEM(bases.shape, jnp.int32),
+            pltpu.VMEM(conv_weight.shape, BF16),
+            pltpu.VMEM(cotangent.shape[1:], BF16),
+            pltpu.VMEM((LINE * n, half), F32),
+            pltpu.SemaphoreType.DMA((3,)),
+        ],
+        space=pltpu.HBM,
+        limit=60,
     )
     got = exchange(sent.reshape(n, LINE // 2, 2, half)).reshape(LINE * n, half)
 
@@ -234,9 +303,16 @@
     gained = [jnp.pad(part, ((0, 4), (0, 0))) for part in pieces(gained, 3)]
     gained = jnp.concatenate(gained, axis=0)
     gram = jnp.dot(stem_weight, stem_weight.T, precision=HIGH) * (1.0 / channels)
-    gram = jnp.concatenate(
-        [jnp.pad(gram, ((0, 4), (0, 4))), jnp.pad(gram, ((4, 0), (4, 0)))], axis=0
-    )
+    tap = jnp.arange(TAPS) // 4
+    ahead, same = tap[None] > tap[:, None], tap[None] == tap[:, None]
+    even = jnp.pad(gram * (2.0 * ahead + same), ((0, 0), (0, 4)))
+    odd = jnp.pad(gram * (2.0 * ahead.T + same), ((0, 0), (4, 0)))
+    ends = jnp.diag(gram)
+    lines = jnp.arange(8 * KW)[:, None]
+    ends = jnp.where(lines == 3, jnp.pad(ends, (0, 4)) * (jnp.arange(24) >= 16), 0.0) + jnp.where(
+        lines == 7, jnp.pad(ends, (4, 0)) * (jnp.arange(24) < 8), 0.0
+    )
+    gram = jnp.concatenate([ends, even[:16], odd[4:]], axis=0)
     gram = jnp.concatenate([part.astype(F32) for part in pieces(gram, 3)], axis=1)
     row = jnp.arange(KW * channels, dtype=jnp.int32)[None, :]
     chosen = (row // share == jnp.arange(n, dtype=jnp.int32)[:, None]).astype(BF16)
@@ -254,18 +330,18 @@
     conv_grad = jnp.concatenate(
         [got[:, ROWS * m : ROWS * m + share].T for m in range(cols)], axis=1
     )
-    mine = jnp.sum(got[:, cols * ROWS : cols * (ROWS + SUMS)], axis=0, keepdims=True)
-    full = exchange(jnp.broadcast_to(mine, (n, mine.shape[1])))
+    mine = call(reduce_kernel, "reduce", jax.ShapeDtypeStruct((n, 128), F32), (got,))
+    full = exchange(mine)
     stem_grad, gain_grad = call(
         finish_kernel,
         "finish",
         (
             jax.ShapeDtypeStruct((TAPS, channels), F32),
-            jax.ShapeDtypeStruct((1, channels), F32),
+            jax.ShapeDtypeStruct((channels,), F32),
         ),
         (full,),
     )
-    return (conv_grad, stem_grad, gain_grad[0])
+    return (conv_grad, stem_grad, gain_grad)
 
 
 def solution(mesh):

time: 86.3 us -> 82.9 us (0.961)
  local copies, waits for them, and re-layouts: 4.14 us -> 1.26 us
  other arithmetic: 2.9 us -> 1.34 us
    unnamed x8 -> x4, local copies, waits for them, and re-layouts: 2.34 us -> 0.01 us
    convert_element_type x1, other arithmetic: 0.9 us -> 0.02 us  [pieces(): top = x.astype(BF16)]
    pallas_call x3 -> x4, Pallas kernels: 10.9 us -> 11.5 us  [call(): pl.pallas_call(kernel, name=name, out_shape=out, in_specs=specs, out_spec...]
where the time goes in v4:
time: 82.9 us; the launch traced here: 82.6 us
  waiting for transfers between devices  26.4 us (32%)
  starting transfers between devices  21.1 us (25%)
  blocking collectives  19 us (23%)
  Pallas kernels  11.5 us (14%)
  other arithmetic  1.34 us (2%)
  local copies, waits for them, and re-layouts  1.26 us (2%)
  matrix products  1.16 us (1%)
  between operations  0.83 us (1%)
    all_to_all x2, waiting for transfers between devices, exchange(): return lax.all_to_all(x, AXES, 0, 0, tiled=True)  26.4 us
    all_to_all x2, starting transfers between devices, exchange(): return lax.all_to_all(x, AXES, 0, 0, tiled=True)  21.1 us
    all_to_all x1, blocking collectives, exchange(): return lax.all_to_all(x, AXES, 0, 0, tiled=True)  19 us
    pallas_call x4, Pallas kernels, call(): pl.pallas_call(kernel, name=name, out_shape=out, in_specs=specs, out_spec...  11.5 us
  transfers between devices with their start and end apart: 2, of which 2 were waited for; matrix products, arithmetic and copies ran while one was open for 5% of the time, Pallas kernels for 0%

profile of v4, /device:TPU:1, one launch (start us, length us, event | category | flops | bytes accessed | tf_op | source)
XLA Modules:
  0.0 82.6 jit_solution(10356180191243925515)
XLA Ops:
  0.6 0.0 copy-start
  0.6 0.0 copy-start.1
  0.7 1.9 %pack.1 = bf16[1536,128]{1,0:T(8,128)(2,1)} custom-call(s32[1,256]{1,0:T(1,128)} %bases_hbm.1, bf16[15,768]{1,0:T(8,128)(2,1)} %weight_hbm.1, bf16[128,768]{1,0:T(8,128)(2,1)} %bitcast.28), custom_call_target="tpu_custom_call" | custom-call | tf_op jit(solution)/shard_map/pack/pallas_call | solution.py:261
  2.6 15.7 %all-to-all-start = ((bf16[256,3,2,128]{3,2,1,0:T(2,128)(2,1)}), bf16[256,3,2,128]{3,2,1,0:T(2,128)(2,1)S(1)}, u32[]{:S(2)}, u32[]{:S(2)}) async-start(bf16[256,3,2,128]{3,2,1,0:T(2,128)(2,1)} %bitcast.27), calls=%async_computation | async-start | bytes 786432 | tf_op jit(solution)/shard_map/all_to_all | solution.py:273
  18.3 1.2 %fusion.20 = (f32[20,20]{1,0:T(8,128)S(1)}, f32[20,20]{1,0:T(8,128)S(1)}, f32[20,20]{1,0:T(8,128)S(1)}) fusion(s32[20]{0:T(128)S(1)} %and_select_fusion, f32[20,768]{1,0:T(8,128)} %stem_ref.1), kind=kOutput, calls=%fused_computation.46 | convolution fusion | flops 3690800 | bytes 66320 | tf_op jit(solution)/shard_map/dot_general | solution.py:305
  19.5 0.8 gather_fusion
  20.3 0.1 compare_select_fusion.1
  20.4 0.1 pad_slice_fusion
  20.5 0.1 select_add_fusion
  20.6 0.0 copy-done.1
  20.6 0.0 copy-done
  20.6 0.3 fusion.chosen_ref
  21.0 0.1 pad_maximum_fusion.2.gram_ref
  21.1 14.3 %all-to-all-done = bf16[256,3,2,128]{3,2,1,0:T(2,128)(2,1)S(1)} async-done(((bf16[256,3,2,128]{3,2,1,0:T(2,128)(2,1)}), bf16[256,3,2,128]{3,2,1,0:T(2,128)(2,1)S(1)}, u32[]{:S(2)}, u32[]{:S(2)}) %all-to-all-start) | async-done | bytes 393248 | tf_op jit(solution)/shard_map/all_to_all | solution.py:273
  35.4 8.1 %main.1 = f32[256,128]{1,0:T(8,128)S(1)} custom-call(s32[1]{0:T(128)} %bitcast.me_ref, bf16[1536,128]{1,0:T(8,128)(2,1)S(1)} %bitcast.24, f32[20,768]{1,0:T(8,128)S(1)} %copy-done, f32[1,768]{1,0:T(1,128)S(1)} %broadcast_in_dim.43.gain_ref, bf16[72,768]{1,0:T(8,128)(2,1)S(1)} %fusion.7.gained_ref, f32[72,72]{1,0:T(8,128)S(1)} %pad_maximum_fusion.2.gram_ref, ...), custom_call_target="tpu_custom_call" | custom-call | tf_op jit(solution)/shard_map/main/pallas_call | solution.py:261
  43.6 19.0 %all_to_all.27 = f32[256,1,128]{2,1,0:T(1,128)S(1)} all-to-all(f32[256,1,128]{2,1,0:T(1,128)S(1)} %bitcast.26), channel_id=1, replica_groups=mesh['seq'=32,'win'=8] {'seq','win'}, dimensions={0} | all-to-all | bytes 262144 | tf_op jit(solution)/shard_map/all_to_all | solution.py:273
  62.6 0.7 reduce.1
  63.3 5.5 %all-to-all-start.2 = ((f32[256,1,128]{2,1,0:T(1,128)}), f32[256,1,128]{2,1,0:T(1,128)S(1)}, u32[]{:S(2)}, u32[]{:S(2)}) async-start(f32[256,1,128]{2,1,0:T(1,128)} %bitcast.12), calls=%async_computation.2 | async-start | bytes 262144 | tf_op jit(solution)/shard_map/all_to_all | solution.py:273
  68.8 0.1 slice_bitcast_fusion.2
  68.9 0.1 copy.25
  69.0 0.1 copy.27
  69.1 0.1 copy.26
  69.1 0.6 pad_maximum_fusion
  69.8 12.1 %all-to-all-done.2 = f32[256,1,128]{2,1,0:T(1,128)S(1)} async-done(((f32[256,1,128]{2,1,0:T(1,128)}), f32[256,1,128]{2,1,0:T(1,128)S(1)}, u32[]{:S(2)}, u32[]{:S(2)}) %all-to-all-start.2) | async-done | bytes 131104 | tf_op jit(solution)/shard_map/all_to_all | solution.py:273
  81.9 0.7 finish.1
  (11 shorter events, 0.1 us)
Async XLA Ops:
  0.6 20.0 %copy-start = (f32[20,768]{1,0:T(8,128)S(1)}, f32[20,768]{1,0:T(8,128)}, u32[]{:S(2)}) copy-start(f32[20,768]{1,0:T(8,128)} %stem_ref.1) | copy-start | bytes 184324
  0.6 19.9 %copy-start.1 = (f32[768]{0:T(1024)S(1)}, f32[768]{0:T(1024)}, u32[]{:S(2)}) copy-start(f32[768]{0:T(1024)} %param.7) | copy-start | bytes 9220
  2.6 32.8 %all-to-all-start = ((bf16[256,3,2,128]{3,2,1,0:T(2,128)(2,1)}), bf16[256,3,2,128]{3,2,1,0:T(2,128)(2,1)S(1)}, u32[]{:S(2)}, u32[]{:S(2)}) async-start(bf16[256,3,2,128]{3,2,1,0:T(2,128)(2,1)} %bitcast.27), calls=%async_computation | async-start | bytes 786432 | tf_op jit(solution)/shard_map/all_to_all | solution.py:273
  63.3 18.6 %all-to-all-start.2 = ((f32[256,1,128]{2,1,0:T(1,128)}), f32[256,1,128]{2,1,0:T(1,128)S(1)}, u32[]{:S(2)}, u32[]{:S(2)}) async-start(f32[256,1,128]{2,1,0:T(1,128)} %bitcast.12), calls=%async_computation.2 | async-start | bytes 262144 | tf_op jit(solution)/shard_map/all_to_all | solution.py:273

commit v5 on v4

--- a/solution.py
+++ b/solution.py
@@ -5,11 +5,12 @@
 from jax import lax
 from jax.experimental import pallas as pl
 from jax.experimental.pallas import tpu as pltpu
-from jax.sharding import PartitionSpec as P
+from jax.sharding import Mesh, PartitionSpec as P
 
 KW = 5
 TAPS = 4 * KW
-AXES = ("seq", "win")
+PLANE = ("row", "win")
+AXES = ("layer",) + PLANE
 F32 = jnp.float32
 BF16 = jnp.bfloat16
 HIGH = lax.Precision.HIGHEST
@@ -17,6 +18,7 @@
 CUBE = 0.044715
 ROWS, SUMS, LINE = 16, 24, 6
 CELLS = 4
+LAYERS = 8
 NN, NT = (((1,), (0,)), ((), ())), (((1,), (1,)), ((), ()))
 
 
@@ -74,9 +76,10 @@
 
 
 def main_kernel(
-    seq, win, me_ref, got_ref, stem_ref, gain_ref, gained_ref, gram_ref, chosen_ref, turn_ref, out_ref, hold
+    layers, seq, win, me_ref, got_ref, stem_ref, gain_ref, gained_ref, gram_ref, chosen_ref, turn_ref, out_ref, hold
 ):
     n = seq * win
+    plane = n // layers
     channels = stem_ref.shape[1]
     cols = channels // n
     hold[: LINE * n, :] = got_ref[...].astype(F32)
@@ -236,17 +239,38 @@
     for m in range(cols):
         rows.append(small[:, m * n : (m + 1) * n] + jnp.where(mine, direct[:, m : m + 1], 0.0))
     rows.append(jnp.zeros((128 - cols * (ROWS + SUMS), n), F32))
-    out_ref[...] = jnp.concatenate(rows, axis=0).T
-
-
-def reduce_kernel(got_ref, out_ref):
-    out_ref[...] = jnp.broadcast_to(jnp.sum(got_ref[...], axis=0, keepdims=True), out_ref.shape)
-
-
-def finish_kernel(got_ref, stem_ref, gain_ref):
+    rows = jnp.concatenate(rows, axis=0).T
+    for layer in range(layers):
+        out_ref[pl.ds(layer, plane, stride=layers), :] = rows[layer * plane : (layer + 1) * plane]
+
+
+def relay_kernel(layers, first, got_ref, out_ref):
+    plane = got_ref.shape[0] // layers
+    total = got_ref[0:layers, :]
+    for source in range(1, plane):
+        total = total + got_ref[source * layers : (source + 1) * layers, :]
+    lane = lax.broadcasted_iota(jnp.int32, total.shape, 1)
+    for layer in range(layers):
+        rows = got_ref[pl.ds(layer, plane, stride=layers), :]
+        at = layer * plane
+        out_ref[at : at + layers, :] = jnp.where(lane < first, rows[:layers], total)
+        out_ref[at + layers : at + plane, :] = rows[layers:]
+
+
+def total_kernel(layers, got_ref, out_ref):
+    plane = got_ref.shape[0] // layers
+    total = got_ref[0:layers, :]
+    for layer in range(1, layers):
+        total = total + got_ref[layer * plane : layer * plane + layers, :]
+    for target in range(plane):
+        out_ref[target * layers : (target + 1) * layers, :] = total
+
+
+def finish_kernel(layers, got_ref, stem_ref, gain_ref):
     n = got_ref.shape[0]
     cols = stem_ref.shape[1] // n
-    turned = got_ref[...].T
+    turned = [got_ref[pl.ds(layer, n // layers, stride=layers), :] for layer in range(layers)]
+    turned = jnp.concatenate(turned, axis=0).T
     for m in range(cols):
         at = ROWS * cols + SUMS * m
         stem_ref[:, m * n : (m + 1) * n] = turned[at : at + TAPS]
@@ -269,18 +293,20 @@
     )(*operands)
 
 
-def exchange(x):
-    return lax.all_to_all(x, AXES, 0, 0, tiled=True)
+def exchange(x, axes):
+    return lax.all_to_all(x, axes, 0, 0, tiled=True)
 
 
 def shards(bases, stem_weight, norm_gain, conv_weight, cotangent):
-    seq, win = lax.axis_size("seq"), lax.axis_size("win")
+    layers, win = lax.axis_size("layer"), lax.axis_size("win")
+    seq = layers * lax.axis_size("row")
     n = seq * win
+    plane = n // layers
     channels = norm_gain.shape[0]
     cols = channels // n
     half = bases.shape[1] // 2
     share = conv_weight.shape[0]
-    me = lax.axis_index("seq") * win + lax.axis_index("win")
+    me = lax.axis_index(AXES)
 
     sent = call(
         functools.partial(pack_kernel, n),
@@ -297,7 +323,7 @@
         space=pltpu.HBM,
         limit=60,
     )
-    got = exchange(sent.reshape(n, LINE // 2, 2, half)).reshape(LINE * n, half)
+    got = exchange(sent.reshape(n, LINE // 2, 2, half), AXES).reshape(LINE * n, half)
 
     gained = stem_weight * norm_gain
     gained = [jnp.pad(part, ((0, 4), (0, 0))) for part in pieces(gained, 3)]
@@ -319,21 +345,24 @@
     turn = (row % share == jnp.arange(ROWS, dtype=jnp.int32)[:, None]).astype(F32)
 
     packed = call(
-        functools.partial(main_kernel, seq, win),
+        functools.partial(main_kernel, layers, seq, win),
         "main",
         jax.ShapeDtypeStruct((n, 128), F32),
         (me.reshape(1), got, stem_weight, norm_gain[None], gained, gram, chosen, turn),
         [pltpu.VMEM((LINE * n + 8, 128), F32)],
         1,
     )
-    got = exchange(packed)
+    shape = jax.ShapeDtypeStruct((n, 128), F32)
+    got = exchange(packed.reshape(plane, layers, 128), PLANE).reshape(n, 128)
+    relayed = call(functools.partial(relay_kernel, layers, cols * ROWS), "relay", shape, (got,))
+    got = exchange(relayed.reshape(layers, plane, 128), "layer").reshape(n, 128)
     conv_grad = jnp.concatenate(
         [got[:, ROWS * m : ROWS * m + share].T for m in range(cols)], axis=1
     )
-    mine = call(reduce_kernel, "reduce", jax.ShapeDtypeStruct((n, 128), F32), (got,))
-    full = exchange(mine)
+    total = call(functools.partial(total_kernel, layers), "total", shape, (got,))
+    full = exchange(total.reshape(plane, layers, 128), PLANE).reshape(n, 128)
     stem_grad, gain_grad = call(
-        finish_kernel,
+        functools.partial(finish_kernel, layers),
         "finish",
         (
             jax.ShapeDtypeStruct((TAPS, channels), F32),
@@ -345,6 +374,10 @@
 
 
 def solution(mesh):
-    in_specs = (P("win", "seq"), P(), P(), P(("seq", "win"), None), P("win", "seq", None))
-    out_specs = (P(("seq", "win"), None), P(), P())
+    seq, win = mesh.devices.shape
+    layers = LAYERS if seq % LAYERS == 0 else 1
+    mesh = Mesh(mesh.devices.reshape(layers, seq // layers, win), AXES)
+    line = ("layer", "row")
+    in_specs = (P("win", line), P(), P(), P(AXES, None), P("win", line, None))
+    out_specs = (P(AXES, None), P(), P())
     return jax.shard_map(shards, mesh=mesh, in_specs=in_specs, out_specs=out_specs, check_vma=False)

time: 82.9 us -> 81.4 us (0.982)
  waiting for transfers between devices: 26.4 us -> 21 us
  blocking collectives: 19 us -> 22.9 us
    all_to_all x2, waiting for transfers between devices: 26.4 us -> 21 us  [exchange(): return lax.all_to_all(x, axes, 0, 0, tiled=True)]
    all_to_all x1 -> x2, blocking collectives: 19 us -> 22.9 us  [exchange(): return lax.all_to_all(x, axes, 0, 0, tiled=True)]
    pallas_call x4 -> x5, Pallas kernels: 11.5 us -> 11.5 us  [call(): pl.pallas_call(kernel, name=name, out_shape=out, in_specs=specs, out_spec...]
where the time goes in v5:
time: 81.4 us; the launch traced here: 81 us
  blocking collectives  22.9 us (28%)
  starting transfers between devices  21 us (26%)
  waiting for transfers between devices  21 us (26%)
  Pallas kernels  11.5 us (14%)
  other arithmetic  1.34 us (2%)
  local copies, waits for them, and re-layouts  1.26 us (2%)
  matrix products  1.16 us (1%)
  between operations  0.84 us (1%)
    all_to_all x2, blocking collectives, exchange(): return lax.all_to_all(x, axes, 0, 0, tiled=True)  22.9 us
    all_to_all x2, starting transfers between devices, exchange(): return lax.all_to_all(x, axes, 0, 0, tiled=True)  21 us
    all_to_all x2, waiting for transfers between devices, exchange(): return lax.all_to_all(x, axes, 0, 0, tiled=True)  21 us
    pallas_call x5, Pallas kernels, call(): pl.pallas_call(kernel, name=name, out_shape=out, in_specs=specs, out_spec...  11.5 us
  transfers between devices with their start and end apart: 2, of which 2 were waited for; matrix products, arithmetic and copies ran while one was open for 5% of the time, Pallas kernels for 0%

profile of v5, /device:TPU:1, one launch (start us, length us, event | category | flops | bytes accessed | tf_op | source)
XLA Modules:
  0.0 81.0 jit_solution(16343815627268945946)
XLA Ops:
  0.6 0.0 copy-start
  0.6 0.0 copy-start.1
  0.7 1.9 %pack.1 = bf16[1536,128]{1,0:T(8,128)(2,1)} custom-call(s32[1,256]{1,0:T(1,128)} %bases_hbm.1, bf16[15,768]{1,0:T(8,128)(2,1)} %weight_hbm.1, bf16[128,768]{1,0:T(8,128)(2,1)} %bitcast.28), custom_call_target="tpu_custom_call" | custom-call | tf_op jit(solution)/shard_map/pack/pallas_call | solution.py:285
  2.6 15.7 %all-to-all-start = ((bf16[256,3,2,128]{3,2,1,0:T(2,128)(2,1)}), bf16[256,3,2,128]{3,2,1,0:T(2,128)(2,1)S(1)}, u32[]{:S(2)}, u32[]{:S(2)}) async-start(bf16[256,3,2,128]{3,2,1,0:T(2,128)(2,1)} %bitcast.27), calls=%async_computation | async-start | bytes 786432 | tf_op jit(solution)/shard_map/all_to_all | solution.py:297
  18.3 1.2 %fusion.20 = (f32[20,20]{1,0:T(8,128)S(1)}, f32[20,20]{1,0:T(8,128)S(1)}, f32[20,20]{1,0:T(8,128)S(1)}) fusion(s32[20]{0:T(128)S(1)} %and_select_fusion, f32[20,768]{1,0:T(8,128)} %stem_ref.1), kind=kOutput, calls=%fused_computation.46 | convolution fusion | flops 3690800 | bytes 66320 | tf_op jit(solution)/shard_map/dot_general | solution.py:331
  19.5 0.8 gather_fusion
  20.3 0.1 compare_select_fusion.1
  20.4 0.1 pad_slice_fusion
  20.5 0.1 select_add_fusion
  20.6 0.0 copy-done.1
  20.6 0.0 copy-done
  20.6 0.3 fusion.chosen_ref
  21.0 0.1 pad_maximum_fusion.2.gram_ref
  21.2 14.3 %all-to-all-done = bf16[256,3,2,128]{3,2,1,0:T(2,128)(2,1)S(1)} async-done(((bf16[256,3,2,128]{3,2,1,0:T(2,128)(2,1)}), bf16[256,3,2,128]{3,2,1,0:T(2,128)(2,1)S(1)}, u32[]{:S(2)}, u32[]{:S(2)}) %all-to-all-start) | async-done | bytes 393248 | tf_op jit(solution)/shard_map/all_to_all | solution.py:297
  35.4 8.1 %main.1 = f32[256,128]{1,0:T(8,128)S(1)} custom-call(s32[1]{0:T(128)} %bitcast.me_ref, bf16[1536,128]{1,0:T(8,128)(2,1)S(1)} %bitcast.22, f32[20,768]{1,0:T(8,128)S(1)} %copy-done, f32[1,768]{1,0:T(1,128)S(1)} %broadcast_in_dim.43.gain_ref, bf16[72,768]{1,0:T(8,128)(2,1)S(1)} %fusion.7.gained_ref, f32[72,72]{1,0:T(8,128)S(1)} %pad_maximum_fusion.2.gram_ref, ...), custom_call_target="tpu_custom_call" | custom-call | tf_op jit(solution)/shard_map/main/pallas_call | solution.py:285
  43.6 12.4 %all_to_all.20 = f32[32,8,128]{2,1,0:T(8,128)S(1)} all-to-all(f32[32,8,128]{2,1,0:T(8,128)S(1)} %bitcast.26), channel_id=1, replica_groups=mesh['layer'=8,'row'=4,'win'=8] {'row','win'}, dimensions={0} | all-to-all | bytes 262144 | tf_op jit(solution)/shard_map/all_to_all | solution.py:297
  56.0 10.6 %all_to_all.21 = f32[8,32,128]{2,1,0:T(8,128)S(1)} all-to-all(f32[8,32,128]{2,1,0:T(8,128)S(1)} %bitcast.25), channel_id=1, replica_groups=mesh['layer'=8,'row'=4,'win'=8] {'layer'}, dimensions={0} | all-to-all | bytes 262144 | tf_op jit(solution)/shard_map/all_to_all | solution.py:297
  66.5 0.7 total.1
  67.2 5.3 %all-to-all-start.3 = ((f32[32,8,128]{2,1,0:T(8,128)}), f32[32,8,128]{2,1,0:T(8,128)S(1)}, u32[]{:S(2)}, u32[]{:S(2)}) async-start(f32[32,8,128]{2,1,0:T(8,128)} %bitcast.12), calls=%async_computation.3 | async-start | bytes 262144 | tf_op jit(solution)/shard_map/all_to_all | solution.py:297
  72.5 0.1 slice_bitcast_fusion.2
  72.7 0.1 copy.20
  72.8 0.1 copy.22
  72.9 0.1 copy.21
  72.9 0.6 pad_maximum_fusion
  73.6 6.7 %all-to-all-done.3 = f32[32,8,128]{2,1,0:T(8,128)S(1)} async-done(((f32[32,8,128]{2,1,0:T(8,128)}), f32[32,8,128]{2,1,0:T(8,128)S(1)}, u32[]{:S(2)}, u32[]{:S(2)}) %all-to-all-start.3) | async-done | bytes 131104 | tf_op jit(solution)/shard_map/all_to_all | solution.py:297
  80.3 0.7 finish.1
  (12 shorter events, 0.2 us)
Async XLA Ops:
  0.6 20.0 %copy-start = (f32[20,768]{1,0:T(8,128)S(1)}, f32[20,768]{1,0:T(8,128)}, u32[]{:S(2)}) copy-start(f32[20,768]{1,0:T(8,128)} %stem_ref.1) | copy-start | bytes 184324
  0.6 19.9 %copy-start.1 = (f32[768]{0:T(1024)S(1)}, f32[768]{0:T(1024)}, u32[]{:S(2)}) copy-start(f32[768]{0:T(1024)} %param.7) | copy-start | bytes 9220
  2.6 32.8 %all-to-all-start = ((bf16[256,3,2,128]{3,2,1,0:T(2,128)(2,1)}), bf16[256,3,2,128]{3,2,1,0:T(2,128)(2,1)S(1)}, u32[]{:S(2)}, u32[]{:S(2)}) async-start(bf16[256,3,2,128]{3,2,1,0:T(2,128)(2,1)} %bitcast.27), calls=%async_computation | async-start | bytes 786432 | tf_op jit(solution)/shard_map/all_to_all | solution.py:297
  67.2 13.1 %all-to-all-start.3 = ((f32[32,8,128]{2,1,0:T(8,128)}), f32[32,8,128]{2,1,0:T(8,128)S(1)}, u32[]{:S(2)}, u32[]{:S(2)}) async-start(f32[32,8,128]{2,1,0:T(8,128)} %bitcast.12), calls=%async_computation.3 | async-start | bytes 262144 | tf_op jit(solution)/shard_map/all_to_all | solution.py:297

commit v6 on v5

--- a/solution.py
+++ b/solution.py
@@ -16,8 +16,9 @@
 HIGH = lax.Precision.HIGHEST
 ROOT = 0.7978845608028654
 CUBE = 0.044715
-ROWS, SUMS, LINE = 16, 24, 6
+ROWS, SUMS, LINE = 16, TAPS + 1, 6
 CELLS = 4
+LAG = 1
 LAYERS = 8
 NN, NT = (((1,), (0,)), ((), ())), (((1,), (1,)), ((), ()))
 
@@ -35,10 +36,10 @@
     return lax.dot_general(a, b, dims, precision=precision, preferred_element_type=F32)
 
 
-def gelu_slope(x):
+def twice_gelu_slope(x):
     sq = x * x
-    th = jnp.tanh(ROOT * x * (1.0 + CUBE * sq))
-    return 0.5 * (1.0 + th) + (0.5 * ROOT) * x * (1.0 - th * th) * (1.0 + 3.0 * CUBE * sq)
+    th = jnp.tanh(x * (ROOT + (ROOT * CUBE) * sq))
+    return (1.0 + th) * (1.0 + (1.0 - th) * (x * (ROOT + (3.0 * ROOT * CUBE) * sq)))
 
 
 def pack_kernel(n, bases_hbm, weight_hbm, cot_hbm, out_ref, bases_ref, weight_ref, cot_ref, hold, sems):
@@ -76,7 +77,7 @@
 
 
 def main_kernel(
-    layers, seq, win, me_ref, got_ref, stem_ref, gain_ref, gained_ref, gram_ref, chosen_ref, turn_ref, out_ref, hold
+    layers, seq, win, me_ref, got_ref, stem_ref, gain_ref, gained_ref, gram_ref, chosen_ref, turn_ref, out_ref, hold, symbols
 ):
     n = seq * win
     plane = n // layers
@@ -87,8 +88,13 @@
     chosen = chosen_ref[...]
     turn = turn_ref[...]
 
-    own = hold[pl.ds(5, n, stride=LINE), :].T[: ROWS * cols]
-    spread = dot(own.astype(BF16), chosen, NN)
+    own = hold[pl.ds(5, n, stride=LINE), :].T[: ROWS * cols].astype(BF16)
+    share, block = KW * channels // n, min(256, channels)
+    spread = []
+    for at in range(0, KW * channels, block):
+        low, high = at // share // 128 * 128, ((at + block - 1) // share // 128 + 1) * 128
+        spread.append(dot(own[:, low:high], chosen[low:high, at : at + block], NN))
+    spread = jnp.concatenate(spread, axis=1)
     line = [
         jnp.sum(spread[ROWS * m : ROWS * (m + 1)] * turn, axis=0, keepdims=True)
         for m in range(cols)
@@ -112,101 +118,118 @@
     width = 128 * CELLS
     count = seq // CELLS
     sub = lax.broadcasted_iota(jnp.int32, (8, 128), 0)
-    lane = lax.broadcasted_iota(jnp.int32, (8, width), 1)
+    lane = lax.broadcasted_iota(jnp.int32, (8, 128), 1)
     wide = lax.broadcasted_iota(jnp.int32, (8, width), 0)
     top = wide < 4
-    first, last = lane == 0, lane == width - 1
+    first, last = lane == 0, lane == 127
     base = (wide % 4).astype(F32)
-
-    def ahead_of(x):
-        return pltpu.roll(x, width - 1, 1)
-
-    def behind_of(x):
-        return pltpu.roll(x, 1, 1)
+    spare, early, low = wide % 4 == 3, wide % 2 == 0, wide % 4 < 2
+
+    def swap(x):
+        return pltpu.roll(x, 4, 0)
+
+    def quad_sum(x):
+        x = x + jnp.where(early, pltpu.roll(x, 7, 0), pltpu.roll(x, 1, 0))
+        return x + jnp.where(low, pltpu.roll(x, 6, 0), pltpu.roll(x, 2, 0))
+
+    def turn_cells(x, by):
+        return [pltpu.roll(x[:, 128 * i : 128 * i + 128], by, 1) for i in range(CELLS)]
+
+    def down(prior, turned):
+        shifted = [0.0 if prior is None else prior[-1]] + turned[:-1]
+        return jnp.concatenate([jnp.where(first, a, b) for a, b in zip(shifted, turned)], axis=1)
+
+    def up(later, turned):
+        shifted = turned[1:] + [0.0 if later is None else later[0]]
+        return jnp.concatenate([jnp.where(last, a, b) for a, b in zip(shifted, turned)], axis=1)
+
+    side = lax.broadcasted_iota(jnp.int32, (win, 128), 1)
+    for parity in range(2):
+        own = hold[pl.ds(3 + parity, n, stride=LINE), :]
+        own = [own[win * s : win * s + win] for s in range(seq)]
+        behind = [-1.0] + [pltpu.roll(x, 1, 1) for x in own]
+        ahead = [pltpu.roll(x, 127, 1) for x in own] + [-1.0]
+        for s in range(seq):
+            symbols[parity, pl.ds(win * s, win), :] = jnp.where(side == 0, behind[s], behind[s + 1])
+            symbols[2 + parity, pl.ds(win * s, win), :] = own[s]
+            symbols[4 + parity, pl.ds(win * s, win), :] = jnp.where(side == 127, ahead[s + 1], ahead[s])
 
     def load(w, c):
-        dr, mid = [], []
+        dr, hots = [], [[], [], []]
         for s in range(c * CELLS, (c + 1) * CELLS):
-            at = LINE * (s * win + w)
-            cell = jnp.where(sub < cols, 0.5 * hold[at : at + 8, :], 0.0)
+            at = s * win + w
+            cell = jnp.where(sub < cols, 0.25 * hold[LINE * at : LINE * at + 8, :], 0.0)
             dr.append(cell + pltpu.roll(cell, 4, 0))
-            mid.append(
-                jnp.where(
-                    sub < 4,
-                    jnp.broadcast_to(hold[at + 3 : at + 4, :], (8, 128)),
-                    jnp.broadcast_to(hold[at + 4 : at + 5, :], (8, 128)),
-                )
-            )
-        mid = jnp.concatenate(mid, axis=1)
-        return jnp.concatenate(dr, axis=1), mid, ahead_of(mid), behind_of(mid)
-
-    def look(prior, cell, later):
-        dr, mid, left, right = cell
-        down = jnp.where(first, -1.0 if prior is None else prior[3], right)
-        up = jnp.where(last, -1.0 if later is None else later[2], left)
-        hots = jnp.concatenate([(x == base).astype(F32) for x in (down, mid, up)], axis=0)
+            for i in range(3):
+                pair = [
+                    jnp.broadcast_to(symbols[2 * i + parity, pl.ds(at, 1), :], (8, 128))
+                    for parity in range(2)
+                ]
+                hots[i].append(jnp.where(sub < 4, *pair))
+        hots = [(jnp.concatenate(x, axis=1) == base).astype(F32) for x in hots]
+        return jnp.concatenate(dr, axis=1), jnp.concatenate(hots, axis=0)
+
+    def look(cell):
+        dr, hots = cell
         narrow = hots.astype(BF16)
         looked = dot(table, jnp.concatenate([narrow] * 3, axis=0), NN)
         taps = [looked[8 * t : 8 * t + 8] for t in range(KW)]
-        mean_e = jnp.sum(looked[40:56] * hots[0:16], axis=0, keepdims=True) + looked[3:4]
-        mean_o = jnp.sum(looked[56:72] * hots[8:24], axis=0, keepdims=True) + looked[7:8]
-        scale_e = lax.rsqrt(mean_e + 1e-06)
-        scale_o = lax.rsqrt(mean_o + 1e-06)
-        scale = jnp.where(top, scale_e, scale_o)
-        swapped = jnp.where(top, scale_o, scale_e)
+        mean_e = looked[40:48] * hots[0:8] + looked[48:56] * hots[8:16]
+        mean_o = looked[56:64] * hots[8:16] + looked[64:72] * hots[16:24]
+        mean = jnp.where(top, mean_e, mean_o) + swap(jnp.where(top, mean_o, mean_e))
+        scale = lax.rsqrt(quad_sum(mean + jnp.where(spare, taps[0], 0.0)) + 1e-06)
+        swapped = swap(scale)
         p0, p2, p4 = taps[0] * scale, taps[2] * scale, taps[4] * scale
         p1, p3 = taps[1] * swapped, taps[3] * swapped
-        down = behind_of(p0 + jnp.where(top, p1, 0.0))
-        up = ahead_of(p4 + jnp.where(top, 0.0, p3))
-        return (p2 + jnp.where(top, p3, p1), up, down), (
-            hots, narrow, taps, scale_e, scale_o, scale, swapped, dr
+        behind = turn_cells(p0 + jnp.where(top, p1, 0.0), 1)
+        ahead = turn_cells(p4 + jnp.where(top, 0.0, p3), 127)
+        return (p2 + jnp.where(top, p3, p1), ahead, behind), (
+            hots, narrow, taps, scale, swapped, dr
         )
 
     def slope(prior, cell, later, dr):
-        pre = cell[0] + jnp.where(first, 0.0 if prior is None else prior[2], cell[2])
-        pre = pre + jnp.where(last, 0.0 if later is None else later[1], cell[1])
-        dpre = dr * gelu_slope(pre)
-        return dpre, ahead_of(dpre), behind_of(dpre)
+        pre = cell[0] + down(prior and prior[2], cell[2]) + up(later and later[1], cell[1])
+        dpre = dr * twice_gelu_slope(pre)
+        return dpre, turn_cells(dpre, 127), turn_cells(dpre, 1)
 
     def close(prior, cell, later, kept):
-        hots, narrow, taps, scale_e, scale_o, scale, swapped, dr = kept
+        hots, narrow, taps, scale, swapped, dr = kept
         dpre = cell[0]
-        ahead = jnp.where(last, 0.0 if later is None else later[1], cell[1])
-        behind = jnp.where(first, 0.0 if prior is None else prior[2], cell[2])
+        ahead = up(later and later[1], cell[1])
+        behind = down(prior and prior[2], cell[2])
         d1 = jnp.where(top, ahead, dpre)
         d3 = jnp.where(top, dpre, behind)
         here = taps[0] * ahead + taps[2] * dpre + taps[4] * behind
         there = taps[1] * d1 + taps[3] * d3
-        both = here + pltpu.roll(there, 4, 0)
-        q_e = jnp.sum(jnp.where(top, both, 0.0), axis=0, keepdims=True)
-        q_o = jnp.sum(jnp.where(top, 0.0, both), axis=0, keepdims=True)
-        u_e = q_e * scale_e * scale_e * scale_e * (1.0 / channels)
-        u_o = q_o * scale_o * scale_o * scale_o * (1.0 / channels)
-        lead = jnp.where(wide == 3, u_e, jnp.where(wide == 7, u_o, ahead * scale))
+        bend = quad_sum(here + swap(there)) * (scale * scale * scale)
+        other = swap(bend)
+        lead = jnp.where(spare, bend, ahead * scale)
         rows = [lead, d1 * swapped, dpre * scale, d3 * swapped, behind * scale, dr]
         rows = jnp.concatenate(rows, axis=0).astype(BF16)
-        u_e, u_o = u_e.astype(BF16) * narrow[0:16], u_o.astype(BF16) * hots[8:24].astype(BF16)
-        return dot(jnp.concatenate([rows, u_e, u_o], axis=0), narrow, NT)
-
-    def at(items, i):
-        return items[i] if 0 <= i < len(items) else None
+        even, odd = jnp.where(top, bend, other), jnp.where(top, other, bend)
+        even = jnp.concatenate([even, even], axis=0).astype(BF16) * narrow[0:16]
+        odd = jnp.concatenate([odd, odd], axis=0).astype(BF16) * hots[8:24].astype(BF16)
+        return dot(jnp.concatenate([rows, even, odd], axis=0), narrow, NT)
 
     total = jnp.zeros((80, 24), F32)
+    jobs = []
     for w in range(win):
-        loaded, looked, kept, slopes = [load(w, 0)], [], [], []
-        for step in range(count + 2):
-            if step + 1 < count:
-                loaded.append(load(w, step + 1))
-            if step < count:
-                part, keep = look(at(loaded, step - 1), loaded[step], at(loaded, step + 1))
-                looked.append(part)
-                kept.append(keep)
-            if 0 <= step - 1 < count:
-                c = step - 1
-                slopes.append(slope(at(looked, c - 1), looked[c], at(looked, c + 1), kept[c][7]))
-            if 0 <= step - 2 < count:
-                c = step - 2
-                total = total + close(at(slopes, c - 1), slopes[c], at(slopes, c + 1), kept[c])
+        jobs += [(w, c) for c in range(count)]
+    looked, kept, slopes = {}, {}, {}
+    for step in range(len(jobs) + LAG + LAG):
+        if step < len(jobs):
+            job = jobs[step]
+            looked[job], kept[job] = look(load(*job))
+        if 0 <= step - LAG < len(jobs):
+            w, c = jobs[step - LAG]
+            slopes[w, c] = slope(
+                looked.get((w, c - 1)), looked[w, c], looked.get((w, c + 1)), kept[w, c][5]
+            )
+        if 0 <= step - LAG - LAG < len(jobs):
+            w, c = jobs[step - LAG - LAG]
+            total = total + close(
+                slopes.get((w, c - 1)), slopes[w, c], slopes.get((w, c + 1)), kept[w, c]
+            )
 
     stem = stem_ref[...]
     gain = gain_ref[...]
@@ -225,56 +248,79 @@
     conv = dot(grads, stem * gain, NN, HIGH)
     conv = jnp.concatenate([conv[4 * t : 4 * t + 4] for t in range(KW)], axis=1)
     conv = jnp.concatenate([conv[m : m + 1] * turn for m in range(cols)], axis=0)
-    conv = dot(jnp.concatenate(pieces(conv, 2), axis=0), chosen, NT)
-    conv = conv[: ROWS * cols] + conv[ROWS * cols :]
+    conv = jnp.concatenate(pieces(conv, 2), axis=0)
+    turned = [jnp.zeros((min(16, n), 2 * ROWS * cols), F32)] * max(1, n // 16)
+    for at in range(0, KW * channels, block):
+        low, high = at // share // 16, (at + block - 1) // share // 16 + 1
+        part = dot(chosen[16 * low : 16 * high, at : at + block], conv[:, at : at + block], NT)
+        for i in range(low, high):
+            turned[i] = turned[i] + part[16 * (i - low) : 16 * (i - low + 1)]
+    turned = jnp.concatenate(turned, axis=0)
+    turned = turned[:, : ROWS * cols] + turned[:, ROWS * cols :]
     back = jnp.zeros((TAPS, channels), F32)
     for part in pieces(grads.T, 3):
         back = back + dot(part, weights, NN)
-    stem_part = gain * back - dot(crossed, stem, NN, HIGH)
+    stem_part = gain * back - dot(crossed * (1.0 / channels), stem, NN, HIGH)
     gain_part = jnp.sum(stem * back, axis=0, keepdims=True)
-    small = jnp.concatenate([stem_part, gain_part, jnp.zeros((3, channels), F32)], axis=0)
-    direct = jnp.concatenate([sums[KW].T, jnp.zeros((4, 4), F32)], axis=0)
+    small = jnp.concatenate([stem_part, gain_part], axis=0)
+    direct = jnp.concatenate([2.0 * sums[KW].T, jnp.zeros((1, 4), F32)], axis=0)
     mine = lax.broadcasted_iota(jnp.int32, (SUMS, n), 1) == me_ref[0]
-    rows = [conv]
+    rows = []
     for m in range(cols):
         rows.append(small[:, m * n : (m + 1) * n] + jnp.where(mine, direct[:, m : m + 1], 0.0))
     rows.append(jnp.zeros((128 - cols * (ROWS + SUMS), n), F32))
-    rows = jnp.concatenate(rows, axis=0).T
+    rows = jnp.concatenate([turned, jnp.concatenate(rows, axis=0).T], axis=1)
     for layer in range(layers):
         out_ref[pl.ds(layer, plane, stride=layers), :] = rows[layer * plane : (layer + 1) * plane]
 
 
-def relay_kernel(layers, first, got_ref, out_ref):
+def relay_kernel(layers, got_ref, out_ref):
     plane = got_ref.shape[0] // layers
+    half = plane // 2
     total = got_ref[0:layers, :]
     for source in range(1, plane):
         total = total + got_ref[source * layers : (source + 1) * layers, :]
+    total = [pltpu.roll(total, 48, 1), pltpu.roll(total, 16, 1)]
+    total += [jnp.zeros((half - 2 * layers, 128), F32)] if half > 2 * layers else []
+    total = jnp.concatenate(total, axis=0)
     lane = lax.broadcasted_iota(jnp.int32, total.shape, 1)
     for layer in range(layers):
         rows = got_ref[pl.ds(layer, plane, stride=layers), :]
-        at = layer * plane
-        out_ref[at : at + layers, :] = jnp.where(lane < first, rows[:layers], total)
-        out_ref[at + layers : at + plane, :] = rows[layers:]
-
-
-def total_kernel(layers, got_ref, out_ref):
-    plane = got_ref.shape[0] // layers
-    total = got_ref[0:layers, :]
-    for layer in range(1, layers):
-        total = total + got_ref[layer * plane : layer * plane + layers, :]
+        pair = jnp.where(lane < 48, rows[:half], pltpu.roll(rows[half:], 48, 1))
+        out_ref[layer * half : (layer + 1) * half, :] = jnp.where(lane < 96, pair, total)
+
+
+def total_kernel(layers, plane, got_ref, out_ref):
+    half = plane // 2
+    parts = []
+    for at in (0, layers):
+        part = got_ref[at : at + layers, :]
+        for layer in range(1, layers):
+            part = part + got_ref[layer * half + at : layer * half + at + layers, :]
+        parts.append(part)
+    lane = lax.broadcasted_iota(jnp.int32, parts[0].shape, 1)
+    total = jnp.where(lane < 32, pltpu.roll(parts[0], 32, 1), pltpu.roll(parts[1], 64, 1))
     for target in range(plane):
         out_ref[target * layers : (target + 1) * layers, :] = total
 
 
-def finish_kernel(layers, got_ref, stem_ref, gain_ref):
-    n = got_ref.shape[0]
+def finish_kernel(layers, conv_ref, small_ref, grad_ref, stem_ref, gain_ref):
+    n = small_ref.shape[0]
+    plane, share = n // layers, grad_ref.shape[0]
+    half = plane // 2
     cols = stem_ref.shape[1] // n
-    turned = [got_ref[pl.ds(layer, n // layers, stride=layers), :] for layer in range(layers)]
-    turned = jnp.concatenate(turned, axis=0).T
+    conv = []
+    for layer in range(layers):
+        cell = conv_ref[layer * half : (layer + 1) * half, :]
+        conv += [cell, pltpu.roll(cell, 128 - 48, 1)]
+    conv = jnp.concatenate(conv, axis=0).T
+    small = [small_ref[pl.ds(layer, plane, stride=layers), :] for layer in range(layers)]
+    small = jnp.concatenate(small, axis=0).T
     for m in range(cols):
-        at = ROWS * cols + SUMS * m
-        stem_ref[:, m * n : (m + 1) * n] = turned[at : at + TAPS]
-        gain_ref[m * n : (m + 1) * n] = turned[at + TAPS]
+        lanes = slice(m * n, (m + 1) * n)
+        grad_ref[:, lanes] = conv[ROWS * m : ROWS * m + share]
+        stem_ref[:, lanes] = small[SUMS * m : SUMS * m + TAPS]
+        gain_ref[lanes] = small[SUMS * m + TAPS]
 
 
 def call(kernel, name, out, operands, scratch=(), smem=0, space=pltpu.VMEM, limit=48):
@@ -349,28 +395,34 @@
         "main",
         jax.ShapeDtypeStruct((n, 128), F32),
         (me.reshape(1), got, stem_weight, norm_gain[None], gained, gram, chosen, turn),
-        [pltpu.VMEM((LINE * n + 8, 128), F32)],
+        [pltpu.VMEM((LINE * n + 8, 128), F32), pltpu.VMEM((6, n, 128), F32)],
         1,
     )
-    shape = jax.ShapeDtypeStruct((n, 128), F32)
     got = exchange(packed.reshape(plane, layers, 128), PLANE).reshape(n, 128)
-    relayed = call(functools.partial(relay_kernel, layers, cols * ROWS), "relay", shape, (got,))
-    got = exchange(relayed.reshape(layers, plane, 128), "layer").reshape(n, 128)
-    conv_grad = jnp.concatenate(
-        [got[:, ROWS * m : ROWS * m + share].T for m in range(cols)], axis=1
-    )
-    total = call(functools.partial(total_kernel, layers), "total", shape, (got,))
-    full = exchange(total.reshape(plane, layers, 128), PLANE).reshape(n, 128)
-    stem_grad, gain_grad = call(
+    relayed = call(
+        functools.partial(relay_kernel, layers),
+        "relay",
+        jax.ShapeDtypeStruct((n // 2, 128), F32),
+        (got,),
+    )
+    conv = exchange(relayed.reshape(layers, plane // 2, 128), "layer").reshape(n // 2, 128)
+    total = call(
+        functools.partial(total_kernel, layers, plane),
+        "total",
+        jax.ShapeDtypeStruct((n, 128), F32),
+        (conv,),
+    )
+    small = exchange(total.reshape(plane, layers, 128), PLANE).reshape(n, 128)
+    return call(
         functools.partial(finish_kernel, layers),
         "finish",
         (
+            jax.ShapeDtypeStruct((share, channels), F32),
             jax.ShapeDtypeStruct((TAPS, channels), F32),
             jax.ShapeDtypeStruct((channels,), F32),
         ),
-        (full,),
-    )
-    return (conv_grad, stem_grad, gain_grad)
+        (conv, small),
+    )
 
 
 def solution(mesh):

time: 81.4 us -> 78.1 us (0.959)
  blocking collectives: 22.9 us -> 34.5 us
  waiting for transfers between devices: 21 us -> 14.3 us
  starting transfers between devices: 21 us -> 15.7 us
  Pallas kernels: 11.5 us -> 9.85 us
    all_to_all x2 -> x3, blocking collectives: 22.9 us -> 34.5 us  [exchange(): return lax.all_to_all(x, axes, 0, 0, tiled=True)]
    all_to_all x2 -> x1, waiting for transfers between devices: 21 us -> 14.3 us  [exchange(): return lax.all_to_all(x, axes, 0, 0, tiled=True)]
    all_to_all x2 -> x1, starting transfers between devices: 21 us -> 15.7 us  [exchange(): return lax.all_to_all(x, axes, 0, 0, tiled=True)]
    pallas_call x5, Pallas kernels: 11.5 us -> 9.85 us  [call(): pl.pallas_call(kernel, name=name, out_shape=out, in_specs=specs, out_spec...]
  transfers between devices with their start and end apart: 2 -> 1, of which waited for: 2 -> 1; matrix products, arithmetic and copies ran while one was open for 5% -> 4% of each run, Pallas kernels for 0% -> 0%
where the time goes in v6:
time: 78.1 us; the launch traced here: 77.8 us
  blocking collectives  34.5 us (44%)
  starting transfers between devices  15.7 us (20%)
  waiting for transfers between devices  14.3 us (18%)
  Pallas kernels  9.85 us (13%)
  matrix products  1.16 us (1%)
  local copies, waits for them, and re-layouts  0.88 us (1%)
  between operations  0.83 us (1%)
    all_to_all x3, blocking collectives, exchange(): return lax.all_to_all(x, axes, 0, 0, tiled=True)  34.5 us
    all_to_all x1, starting transfers between devices, exchange(): return lax.all_to_all(x, axes, 0, 0, tiled=True)  15.7 us
    all_to_all x1, waiting for transfers between devices, exchange(): return lax.all_to_all(x, axes, 0, 0, tiled=True)  14.3 us
    pallas_call x5, Pallas kernels, call(): pl.pallas_call(kernel, name=name, out_shape=out, in_specs=specs, out_spec...  9.85 us
  transfers between devices with their start and end apart: 1, of which 1 were waited for; matrix products, arithmetic and copies ran while one was open for 4% of the time, Pallas kernels for 0%

profile of v6, /device:TPU:1, one launch (start us, length us, event | category | flops | bytes accessed | tf_op | source)
XLA Modules:
  0.0 77.8 jit_solution(5619987631566610414)
XLA Ops:
  0.6 0.0 copy-start
  0.6 0.0 copy-start.1
  0.7 1.9 %pack.1 = bf16[1536,128]{1,0:T(8,128)(2,1)} custom-call(s32[1,256]{1,0:T(1,128)} %bases_hbm.1, bf16[15,768]{1,0:T(8,128)(2,1)} %weight_hbm.1, bf16[128,768]{1,0:T(8,128)(2,1)} %bitcast.23), custom_call_target="tpu_custom_call" | custom-call | tf_op jit(solution)/shard_map/pack/pallas_call | solution.py:331
  2.6 15.7 %all-to-all-start = ((bf16[256,3,2,128]{3,2,1,0:T(2,128)(2,1)}), bf16[256,3,2,128]{3,2,1,0:T(2,128)(2,1)S(1)}, u32[]{:S(2)}, u32[]{:S(2)}) async-start(bf16[256,3,2,128]{3,2,1,0:T(2,128)(2,1)} %bitcast.22), calls=%async_computation | async-start | bytes 786432 | tf_op jit(solution)/shard_map/all_to_all | solution.py:343
  18.3 1.2 %fusion.20 = (f32[20,20]{1,0:T(8,128)S(1)}, f32[20,20]{1,0:T(8,128)S(1)}, f32[20,20]{1,0:T(8,128)S(1)}) fusion(s32[20]{0:T(128)S(1)} %and_select_fusion, f32[20,768]{1,0:T(8,128)} %stem_ref.1), kind=kOutput, calls=%fused_computation.42 | convolution fusion | flops 3690800 | bytes 66320 | tf_op jit(solution)/shard_map/dot_general | solution.py:377
  19.5 0.8 %gather_fusion = f32[20]{0:T(128)S(1)} fusion(f32[20,20]{1,0:T(8,128)S(1)} %get-tuple-element.12, s32[20]{0:T(128)S(1)} %or_bitcast_fusion), kind=kCustom, calls=%fused_computation | custom fusion | bytes 320 | tf_op jit(solution)/shard_map/jit(_diag)/jit(diagonal)/cond/branch_0_fun/gather | solution.py:382
  20.3 0.1 compare_select_fusion.1
  20.4 0.1 pad_slice_fusion
  20.5 0.1 select_add_fusion
  20.6 0.0 copy-done.1
  20.6 0.0 copy-done
  20.6 0.3 fusion.chosen_ref
  21.0 0.1 pad_maximum_fusion.1.gram_ref
  21.1 14.3 %all-to-all-done = bf16[256,3,2,128]{3,2,1,0:T(2,128)(2,1)S(1)} async-done(((bf16[256,3,2,128]{3,2,1,0:T(2,128)(2,1)}), bf16[256,3,2,128]{3,2,1,0:T(2,128)(2,1)S(1)}, u32[]{:S(2)}, u32[]{:S(2)}) %all-to-all-start) | async-done | bytes 393248 | tf_op jit(solution)/shard_map/all_to_all | solution.py:343
  35.4 6.9 %main.1 = f32[256,128]{1,0:T(8,128)S(1)} custom-call(s32[1]{0:T(128)} %bitcast.me_ref, bf16[1536,128]{1,0:T(8,128)(2,1)S(1)} %bitcast.14, f32[20,768]{1,0:T(8,128)S(1)} %copy-done, f32[1,768]{1,0:T(1,128)S(1)} %broadcast_in_dim.43.gain_ref, bf16[72,768]{1,0:T(8,128)(2,1)S(1)} %fusion.7.gained_ref, f32[72,72]{1,0:T(8,128)S(1)} %pad_maximum_fusion.1.gram_ref, ...), custom_call_target="tpu_custom_call" | custom-call | tf_op jit(solution)/shard_map/main/pallas_call | solution.py:331
  42.3 12.4 %all_to_all.20 = f32[32,8,128]{2,1,0:T(8,128)S(1)} all-to-all(f32[32,8,128]{2,1,0:T(8,128)S(1)} %bitcast.20), channel_id=1, replica_groups=mesh['layer'=8,'row'=4,'win'=8] {'row','win'}, dimensions={0} | all-to-all | bytes 262144 | tf_op jit(solution)/shard_map/all_to_all | solution.py:343
  54.7 0.1 relay.1
  54.8 9.6 %all_to_all.21 = f32[8,16,128]{2,1,0:T(8,128)S(1)} all-to-all(f32[8,16,128]{2,1,0:T(8,128)S(1)} %bitcast.21), channel_id=1, replica_groups=mesh['layer'=8,'row'=4,'win'=8] {'layer'}, dimensions={0} | all-to-all | bytes 131072 | tf_op jit(solution)/shard_map/all_to_all | solution.py:343
  64.4 0.1 total.1
  64.5 12.5 %all_to_all.22 = f32[32,8,128]{2,1,0:T(8,128)S(1)} all-to-all(f32[32,8,128]{2,1,0:T(8,128)S(1)} %bitcast.19), channel_id=1, replica_groups=mesh['layer'=8,'row'=4,'win'=8] {'row','win'}, dimensions={0} | all-to-all | bytes 262144 | tf_op jit(solution)/shard_map/all_to_all | solution.py:343
  77.0 0.8 %finish.1 = (f32[15,768]{1,0:T(8,128)}, f32[20,768]{1,0:T(8,128)}, f32[768]{0:T(1024)}) custom-call(f32[128,128]{1,0:T(8,128)S(1)} %bitcast.16, f32[256,128]{1,0:T(8,128)S(1)} %bitcast.17), custom_call_target="tpu_custom_call" | custom-call | tf_op jit(solution)/shard_map/finish/pallas_call | solution.py:331
  (11 shorter events, 0.1 us)
Async XLA Ops:
  0.6 20.0 %copy-start = (f32[20,768]{1,0:T(8,128)S(1)}, f32[20,768]{1,0:T(8,128)}, u32[]{:S(2)}) copy-start(f32[20,768]{1,0:T(8,128)} %stem_ref.1) | copy-start | bytes 184324
  0.6 19.9 %copy-start.1 = (f32[768]{0:T(1024)S(1)}, f32[768]{0:T(1024)}, u32[]{:S(2)}) copy-start(f32[768]{0:T(1024)} %param.7) | copy-start | bytes 9220
  2.6 32.8 %all-to-all-start = ((bf16[256,3,2,128]{3,2,1,0:T(2,128)(2,1)}), bf16[256,3,2,128]{3,2,1,0:T(2,128)(2,1)S(1)}, u32[]{:S(2)}, u32[]{:S(2)}) async-start(bf16[256,3,2,128]{3,2,1,0:T(2,128)(2,1)} %bitcast.22), calls=%async_computation | async-start | bytes 786432 | tf_op jit(solution)/shard_map/all_to_all | solution.py:343

commit v7 on v6

--- a/solution.py
+++ b/solution.py
@@ -158,7 +158,7 @@
         dr, hots = [], [[], [], []]
         for s in range(c * CELLS, (c + 1) * CELLS):
             at = s * win + w
-            cell = jnp.where(sub < cols, 0.25 * hold[LINE * at : LINE * at + 8, :], 0.0)
+            cell = jnp.where(sub < cols, hold[LINE * at : LINE * at + 8, :], 0.0)
             dr.append(cell + pltpu.roll(cell, 4, 0))
             for i in range(3):
                 pair = [
@@ -166,7 +166,7 @@
                     for parity in range(2)
                 ]
                 hots[i].append(jnp.where(sub < 4, *pair))
-        hots = [(jnp.concatenate(x, axis=1) == base).astype(F32) for x in hots]
+        hots = [jnp.maximum(1.0 - jnp.abs(jnp.concatenate(x, axis=1) - base), 0.0) for x in hots]
         return jnp.concatenate(dr, axis=1), jnp.concatenate(hots, axis=0)
 
     def look(cell):
@@ -177,7 +177,8 @@
         mean_e = looked[40:48] * hots[0:8] + looked[48:56] * hots[8:16]
         mean_o = looked[56:64] * hots[8:16] + looked[64:72] * hots[16:24]
         mean = jnp.where(top, mean_e, mean_o) + swap(jnp.where(top, mean_o, mean_e))
-        scale = lax.rsqrt(quad_sum(mean + jnp.where(spare, taps[0], 0.0)) + 1e-06)
+        mean = quad_sum(mean + jnp.where(spare, taps[0], 0.0))
+        scale = lax.rsqrt(jnp.maximum(mean, 0.0) + 1e-06)
         swapped = swap(scale)
         p0, p2, p4 = taps[0] * scale, taps[2] * scale, taps[4] * scale
         p1, p3 = taps[1] * swapped, taps[3] * swapped
@@ -201,15 +202,15 @@
         d3 = jnp.where(top, dpre, behind)
         here = taps[0] * ahead + taps[2] * dpre + taps[4] * behind
         there = taps[1] * d1 + taps[3] * d3
-        bend = quad_sum(here + swap(there)) * (scale * scale * scale)
-        other = swap(bend)
+        bend = here + swap(there)
+        bend = pltpu.roll(bend, 1, 0) + pltpu.roll(bend, 2, 0) + pltpu.roll(bend, 3, 0)
+        bend = bend * (scale * scale * scale)
         lead = jnp.where(spare, bend, ahead * scale)
         rows = [lead, d1 * swapped, dpre * scale, d3 * swapped, behind * scale, dr]
-        rows = jnp.concatenate(rows, axis=0).astype(BF16)
-        even, odd = jnp.where(top, bend, other), jnp.where(top, other, bend)
-        even = jnp.concatenate([even, even], axis=0).astype(BF16) * narrow[0:16]
-        odd = jnp.concatenate([odd, odd], axis=0).astype(BF16) * hots[8:24].astype(BF16)
-        return dot(jnp.concatenate([rows, even, odd], axis=0), narrow, NT)
+        even = jnp.broadcast_to(bend[3:4], bend.shape)
+        odd = jnp.broadcast_to(bend[7:8], bend.shape)
+        rows += [even * hots[0:8], even * hots[8:16], odd * hots[8:16], odd * hots[16:24]]
+        return dot(jnp.concatenate(rows, axis=0), hots, NT)
 
     total = jnp.zeros((80, 24), F32)
     jobs = []
@@ -233,6 +234,7 @@
 
     stem = stem_ref[...]
     gain = gain_ref[...]
+    total = 0.25 * total
     sums = []
     for t in range(KW + 1):
         cell = total[8 * t : 8 * t + 8]

time: 78.1 us -> 77.6 us (level)
  no operation moved by 1% of the time
where the time goes in v7:
time: 77.6 us; the launch traced here: 77.3 us
  blocking collectives  34.5 us (44%)
  starting transfers between devices  15.7 us (20%)
  waiting for transfers between devices  14.3 us (18%)
  Pallas kernels  9.3 us (12%)
  matrix products  1.16 us (1%)
  local copies, waits for them, and re-layouts  0.88 us (1%)
  between operations  0.83 us (1%)
    all_to_all x3, blocking collectives, exchange(): return lax.all_to_all(x, axes, 0, 0, tiled=True)  34.5 us
    all_to_all x1, starting transfers between devices, exchange(): return lax.all_to_all(x, axes, 0, 0, tiled=True)  15.7 us
    all_to_all x1, waiting for transfers between devices, exchange(): return lax.all_to_all(x, axes, 0, 0, tiled=True)  14.3 us
    pallas_call x5, Pallas kernels, call(): pl.pallas_call(kernel, name=name, out_shape=out, in_specs=specs, out_spec...  9.3 us
  transfers between devices with their start and end apart: 1, of which 1 were waited for; matrix products, arithmetic and copies ran while one was open for 4% of the time, Pallas kernels for 0%

profile of v7, /device:TPU:1, one launch (start us, length us, event | category | flops | bytes accessed | tf_op | source)
XLA Modules:
  0.0 77.3 jit_solution(16736000935988399604)
XLA Ops:
  0.6 0.0 copy-start
  0.6 0.0 copy-start.1
  0.7 1.9 %pack.1 = bf16[1536,128]{1,0:T(8,128)(2,1)} custom-call(s32[1,256]{1,0:T(1,128)} %bases_hbm.1, bf16[15,768]{1,0:T(8,128)(2,1)} %weight_hbm.1, bf16[128,768]{1,0:T(8,128)(2,1)} %bitcast.23), custom_call_target="tpu_custom_call" | custom-call | tf_op jit(solution)/shard_map/pack/pallas_call | solution.py:333
  2.6 15.7 %all-to-all-start = ((bf16[256,3,2,128]{3,2,1,0:T(2,128)(2,1)}), bf16[256,3,2,128]{3,2,1,0:T(2,128)(2,1)S(1)}, u32[]{:S(2)}, u32[]{:S(2)}) async-start(bf16[256,3,2,128]{3,2,1,0:T(2,128)(2,1)} %bitcast.22), calls=%async_computation | async-start | bytes 786432 | tf_op jit(solution)/shard_map/all_to_all | solution.py:345
  18.3 1.2 %fusion.20 = (f32[20,20]{1,0:T(8,128)S(1)}, f32[20,20]{1,0:T(8,128)S(1)}, f32[20,20]{1,0:T(8,128)S(1)}) fusion(s32[20]{0:T(128)S(1)} %and_select_fusion, f32[20,768]{1,0:T(8,128)} %stem_ref.1), kind=kOutput, calls=%fused_computation.42 | convolution fusion | flops 3690800 | bytes 66320 | tf_op jit(solution)/shard_map/dot_general | solution.py:379
  19.5 0.8 %gather_fusion = f32[20]{0:T(128)S(1)} fusion(f32[20,20]{1,0:T(8,128)S(1)} %get-tuple-element.12, s32[20]{0:T(128)S(1)} %or_bitcast_fusion), kind=kCustom, calls=%fused_computation | custom fusion | bytes 320 | tf_op jit(solution)/shard_map/jit(_diag)/jit(diagonal)/cond/branch_0_fun/gather | solution.py:384
  20.3 0.1 compare_select_fusion.1
  20.4 0.1 pad_slice_fusion
  20.5 0.1 select_add_fusion
  20.6 0.0 copy-done.1
  20.6 0.0 copy-done
  20.6 0.3 fusion.chosen_ref
  21.0 0.1 pad_maximum_fusion.1.gram_ref
  21.1 14.3 %all-to-all-done = bf16[256,3,2,128]{3,2,1,0:T(2,128)(2,1)S(1)} async-done(((bf16[256,3,2,128]{3,2,1,0:T(2,128)(2,1)}), bf16[256,3,2,128]{3,2,1,0:T(2,128)(2,1)S(1)}, u32[]{:S(2)}, u32[]{:S(2)}) %all-to-all-start) | async-done | bytes 393248 | tf_op jit(solution)/shard_map/all_to_all | solution.py:345
  35.4 6.3 %main.1 = f32[256,128]{1,0:T(8,128)S(1)} custom-call(s32[1]{0:T(128)} %bitcast.me_ref, bf16[1536,128]{1,0:T(8,128)(2,1)S(1)} %bitcast.14, f32[20,768]{1,0:T(8,128)S(1)} %copy-done, f32[1,768]{1,0:T(1,128)S(1)} %broadcast_in_dim.43.gain_ref, bf16[72,768]{1,0:T(8,128)(2,1)S(1)} %fusion.7.gained_ref, f32[72,72]{1,0:T(8,128)S(1)} %pad_maximum_fusion.1.gram_ref, ...), custom_call_target="tpu_custom_call" | custom-call | tf_op jit(solution)/shard_map/main/pallas_call | solution.py:333
  41.8 12.4 %all_to_all.20 = f32[32,8,128]{2,1,0:T(8,128)S(1)} all-to-all(f32[32,8,128]{2,1,0:T(8,128)S(1)} %bitcast.20), channel_id=1, replica_groups=mesh['layer'=8,'row'=4,'win'=8] {'row','win'}, dimensions={0} | all-to-all | bytes 262144 | tf_op jit(solution)/shard_map/all_to_all | solution.py:345
  54.1 0.1 relay.1
  54.3 9.6 %all_to_all.21 = f32[8,16,128]{2,1,0:T(8,128)S(1)} all-to-all(f32[8,16,128]{2,1,0:T(8,128)S(1)} %bitcast.21), channel_id=1, replica_groups=mesh['layer'=8,'row'=4,'win'=8] {'layer'}, dimensions={0} | all-to-all | bytes 131072 | tf_op jit(solution)/shard_map/all_to_all | solution.py:345
  63.8 0.1 total.1
  63.9 12.5 %all_to_all.22 = f32[32,8,128]{2,1,0:T(8,128)S(1)} all-to-all(f32[32,8,128]{2,1,0:T(8,128)S(1)} %bitcast.19), channel_id=1, replica_groups=mesh['layer'=8,'row'=4,'win'=8] {'row','win'}, dimensions={0} | all-to-all | bytes 262144 | tf_op jit(solution)/shard_map/all_to_all | solution.py:345
  76.4 0.8 %finish.1 = (f32[15,768]{1,0:T(8,128)}, f32[20,768]{1,0:T(8,128)}, f32[768]{0:T(1024)}) custom-call(f32[128,128]{1,0:T(8,128)S(1)} %bitcast.16, f32[256,128]{1,0:T(8,128)S(1)} %bitcast.17), custom_call_target="tpu_custom_call" | custom-call | tf_op jit(solution)/shard_map/finish/pallas_call | solution.py:333
  (11 shorter events, 0.1 us)
Async XLA Ops:
  0.6 20.0 %copy-start = (f32[20,768]{1,0:T(8,128)S(1)}, f32[20,768]{1,0:T(8,128)}, u32[]{:S(2)}) copy-start(f32[20,768]{1,0:T(8,128)} %stem_ref.1) | copy-start | bytes 184324
  0.6 19.9 %copy-start.1 = (f32[768]{0:T(1024)S(1)}, f32[768]{0:T(1024)}, u32[]{:S(2)}) copy-start(f32[768]{0:T(1024)} %param.7) | copy-start | bytes 9220
  2.6 32.8 %all-to-all-start = ((bf16[256,3,2,128]{3,2,1,0:T(2,128)(2,1)}), bf16[256,3,2,128]{3,2,1,0:T(2,128)(2,1)S(1)}, u32[]{:S(2)}, u32[]{:S(2)}) async-start(bf16[256,3,2,128]{3,2,1,0:T(2,128)(2,1)} %bitcast.22), calls=%async_computation | async-start | bytes 786432 | tf_op jit(solution)/shard_map/all_to_all | solution.py:345

commit v8 on v7

--- a/solution.py
+++ b/solution.py
@@ -17,7 +17,7 @@
 ROOT = 0.7978845608028654
 CUBE = 0.044715
 ROWS, SUMS, LINE = 16, TAPS + 1, 6
-CELLS = 4
+CELLS = 2
 LAG = 1
 LAYERS = 8
 NN, NT = (((1,), (0,)), ((), ())), (((1,), (1,)), ((), ()))
@@ -34,6 +34,13 @@
 
 def dot(a, b, dims, precision=None):
     return lax.dot_general(a, b, dims, precision=precision, preferred_element_type=F32)
+
+
+def split_dot(a, b_ref):
+    blank = jnp.zeros((a.shape[0], 4), F32)
+    big, small = [jnp.concatenate([x.astype(F32), blank], axis=1) for x in pieces(a, 2)]
+    left = jnp.concatenate([big, big, big, small, small], axis=1).astype(BF16)
+    return dot(left, jnp.concatenate([b_ref[...], b_ref[:48]], axis=0), NN)
 
 
 def twice_gelu_slope(x):
@@ -77,7 +84,7 @@
 
 
 def main_kernel(
-    layers, seq, win, me_ref, got_ref, stem_ref, gain_ref, gained_ref, gram_ref, chosen_ref, turn_ref, out_ref, hold, symbols
+    layers, seq, win, me_ref, got_ref, stem_ref, gain_ref, parts_ref, gained_ref, gram_ref, chosen_ref, turn_ref, out_ref, hold, symbols
 ):
     n = seq * win
     plane = n // layers
@@ -112,8 +119,7 @@
         pair = [jnp.concatenate([tap, blank], axis=1), jnp.concatenate([blank, tap], axis=1)]
         table += pair if t % 2 == 0 else pair[::-1]
     table = [part.astype(F32) for part in pieces(jnp.concatenate(table, axis=0), 3)]
-    table = jnp.concatenate([jnp.concatenate(table, axis=1), jnp.zeros((32, 72), F32)], axis=0)
-    table = (table + gram_ref[...]).astype(BF16)
+    table = jnp.concatenate([jnp.concatenate(table, axis=1), gram_ref[...]], axis=0).astype(BF16)
 
     width = 128 * CELLS
     count = seq // CELLS
@@ -123,7 +129,7 @@
     top = wide < 4
     first, last = lane == 0, lane == 127
     base = (wide % 4).astype(F32)
-    spare, early, low = wide % 4 == 3, wide % 2 == 0, wide % 4 < 2
+    early, low = wide % 2 == 0, wide % 4 < 2
 
     def swap(x):
         return pltpu.roll(x, 4, 0)
@@ -177,8 +183,7 @@
         mean_e = looked[40:48] * hots[0:8] + looked[48:56] * hots[8:16]
         mean_o = looked[56:64] * hots[8:16] + looked[64:72] * hots[16:24]
         mean = jnp.where(top, mean_e, mean_o) + swap(jnp.where(top, mean_o, mean_e))
-        mean = quad_sum(mean + jnp.where(spare, taps[0], 0.0))
-        scale = lax.rsqrt(jnp.maximum(mean, 0.0) + 1e-06)
+        scale = lax.rsqrt(jnp.maximum(quad_sum(mean), 0.0) + 1e-06)
         swapped = swap(scale)
         p0, p2, p4 = taps[0] * scale, taps[2] * scale, taps[4] * scale
         p1, p3 = taps[1] * swapped, taps[3] * swapped
@@ -205,8 +210,7 @@
         bend = here + swap(there)
         bend = pltpu.roll(bend, 1, 0) + pltpu.roll(bend, 2, 0) + pltpu.roll(bend, 3, 0)
         bend = bend * (scale * scale * scale)
-        lead = jnp.where(spare, bend, ahead * scale)
-        rows = [lead, d1 * swapped, dpre * scale, d3 * swapped, behind * scale, dr]
+        rows = [ahead * scale, d1 * swapped, dpre * scale, d3 * swapped, behind * scale, dr]
         even = jnp.broadcast_to(bend[3:4], bend.shape)
         odd = jnp.broadcast_to(bend[7:8], bend.shape)
         rows += [even * hots[0:8], even * hots[8:16], odd * hots[8:16], odd * hots[16:24]]
@@ -243,11 +247,11 @@
     grads = jnp.concatenate(sums[:KW], axis=0)
     even, odd = total[48:64, :TAPS], total[64:80, 4:]
     same = lax.broadcasted_iota(jnp.int32, (4, 4), 0) == lax.broadcasted_iota(jnp.int32, (4, 4), 1)
-    even_end = [even[:, 16:].T, jnp.where(same, total[3:4, 16:TAPS], 0.0)]
-    odd_end = [jnp.where(same, total[7:8, 4:8], 0.0), odd[:, :4].T]
+    even_end = [even[:, 16:].T, jnp.where(same, jnp.sum(even[12:16, 16:], axis=0, keepdims=True), 0.0)]
+    odd_end = [jnp.where(same, jnp.sum(odd[0:4, :4], axis=0, keepdims=True), 0.0), odd[:, :4].T]
     crossed = jnp.concatenate([even, jnp.concatenate(even_end, axis=1)], axis=0)
     crossed = crossed + jnp.concatenate([jnp.concatenate(odd_end, axis=1), odd], axis=0)
-    conv = dot(grads, stem * gain, NN, HIGH)
+    conv = split_dot(grads, gained_ref)
     conv = jnp.concatenate([conv[4 * t : 4 * t + 4] for t in range(KW)], axis=1)
     conv = jnp.concatenate([conv[m : m + 1] * turn for m in range(cols)], axis=0)
     conv = jnp.concatenate(pieces(conv, 2), axis=0)
@@ -262,7 +266,7 @@
     back = jnp.zeros((TAPS, channels), F32)
     for part in pieces(grads.T, 3):
         back = back + dot(part, weights, NN)
-    stem_part = gain * back - dot(crossed * (1.0 / channels), stem, NN, HIGH)
+    stem_part = gain * back - split_dot(crossed * (1.0 / channels), parts_ref)
     gain_part = jnp.sum(stem * back, axis=0, keepdims=True)
     small = jnp.concatenate([stem_part, gain_part], axis=0)
     direct = jnp.concatenate([2.0 * sums[KW].T, jnp.zeros((1, 4), F32)], axis=0)
@@ -373,20 +377,18 @@
     )
     got = exchange(sent.reshape(n, LINE // 2, 2, half), AXES).reshape(LINE * n, half)
 
-    gained = stem_weight * norm_gain
-    gained = [jnp.pad(part, ((0, 4), (0, 0))) for part in pieces(gained, 3)]
-    gained = jnp.concatenate(gained, axis=0)
+    parts, gained = [
+        jnp.concatenate([jnp.pad(part, ((0, 4), (0, 0))) for part in pieces(x, 3)], axis=0)
+        for x in (stem_weight, stem_weight * norm_gain)
+    ]
     gram = jnp.dot(stem_weight, stem_weight.T, precision=HIGH) * (1.0 / channels)
     tap = jnp.arange(TAPS) // 4
     ahead, same = tap[None] > tap[:, None], tap[None] == tap[:, None]
-    even = jnp.pad(gram * (2.0 * ahead + same), ((0, 0), (0, 4)))
-    odd = jnp.pad(gram * (2.0 * ahead.T + same), ((0, 0), (4, 0)))
-    ends = jnp.diag(gram)
-    lines = jnp.arange(8 * KW)[:, None]
-    ends = jnp.where(lines == 3, jnp.pad(ends, (0, 4)) * (jnp.arange(24) >= 16), 0.0) + jnp.where(
-        lines == 7, jnp.pad(ends, (4, 0)) * (jnp.arange(24) < 8), 0.0
-    )
-    gram = jnp.concatenate([ends, even[:16], odd[4:]], axis=0)
+    square = jnp.diag(gram)[None]
+    even = gram * (2.0 * ahead + same) + square * ((tap[:, None] == 3) & (tap[None] == 4))
+    odd = gram * (2.0 * ahead.T + same) + square * ((tap[:, None] == 1) & (tap[None] == 0))
+    even, odd = jnp.pad(even[:16], ((0, 0), (0, 4))), jnp.pad(odd[4:], ((0, 0), (4, 0)))
+    gram = jnp.concatenate([even, odd], axis=0)
     gram = jnp.concatenate([part.astype(F32) for part in pieces(gram, 3)], axis=1)
     row = jnp.arange(KW * channels, dtype=jnp.int32)[None, :]
     chosen = (row // share == jnp.arange(n, dtype=jnp.int32)[:, None]).astype(BF16)
@@ -396,7 +398,7 @@
         functools.partial(main_kernel, layers, seq, win),
         "main",
         jax.ShapeDtypeStruct((n, 128), F32),
-        (me.reshape(1), got, stem_weight, norm_gain[None], gained, gram, chosen, turn),
+        (me.reshape(1), got, stem_weight, norm_gain[None], parts, gained, gram, chosen, turn),
         [pltpu.VMEM((LINE * n + 8, 128), F32), pltpu.VMEM((6, n, 128), F32)],
         1,
     )

time: 77.6 us -> 77.4 us (level)
  no operation moved by 1% of the time
where the time goes in v8:
time: 77.4 us; the launch traced here: 77.1 us
  blocking collectives  34.5 us (45%)
  starting transfers between devices  15.7 us (20%)
  waiting for transfers between devices  14.1 us (18%)
  Pallas kernels  9.09 us (12%)
  matrix products  1.16 us (1%)
  local copies, waits for them, and re-layouts  0.95 us (1%)
  other arithmetic  0.85 us (1%)
  between operations  0.79 us (1%)
    all_to_all x3, blocking collectives, exchange(): return lax.all_to_all(x, axes, 0, 0, tiled=True)  34.5 us
    all_to_all x1, starting transfers between devices, exchange(): return lax.all_to_all(x, axes, 0, 0, tiled=True)  15.7 us
    all_to_all x1, waiting for transfers between devices, exchange(): return lax.all_to_all(x, axes, 0, 0, tiled=True)  14.1 us
    pallas_call x5, Pallas kernels, call(): pl.pallas_call(kernel, name=name, out_shape=out, in_specs=specs, out_spec...  9.09 us
  transfers between devices with their start and end apart: 1, of which 1 were waited for; matrix products, arithmetic and copies ran while one was open for 4% of the time, Pallas kernels for 0%

profile of v8, /device:TPU:1, one launch (start us, length us, event | category | flops | bytes accessed | tf_op | source)
XLA Modules:
  0.0 77.1 jit_solution(6349521719992830864)
XLA Ops:
  0.6 0.0 copy-start
  0.6 0.0 copy-start.1
  0.7 1.9 %pack.1 = bf16[1536,128]{1,0:T(8,128)(2,1)} custom-call(s32[1,256]{1,0:T(1,128)} %bases_hbm.1, bf16[15,768]{1,0:T(8,128)(2,1)} %weight_hbm.1, bf16[128,768]{1,0:T(8,128)(2,1)} %bitcast.24), custom_call_target="tpu_custom_call" | custom-call | tf_op jit(solution)/shard_map/pack/pallas_call | solution.py:337
  2.6 15.7 %all-to-all-start = ((bf16[256,3,2,128]{3,2,1,0:T(2,128)(2,1)}), bf16[256,3,2,128]{3,2,1,0:T(2,128)(2,1)S(1)}, u32[]{:S(2)}, u32[]{:S(2)}) async-start(bf16[256,3,2,128]{3,2,1,0:T(2,128)(2,1)} %bitcast.23), calls=%async_computation | async-start | bytes 786432 | tf_op jit(solution)/shard_map/all_to_all | solution.py:349
  18.3 0.1 fusion.28
  18.4 0.1 compare_convert_fusion
  18.5 0.1 slice.16
  18.6 1.2 %convolution_multiply_fusion = f32[20,20]{1,0:T(8,128)S(1)} fusion(f32[20,768]{1,0:T(8,128)} %stem_ref.1), kind=kOutput, calls=%fused_computation.3 | convolution fusion | flops 3686800 | bytes 63040 | tf_op jit(solution)/shard_map/dot_general | solution.py:384
  19.8 0.8 %gather_fusion = f32[20]{0:T(128)S(1)} fusion(f32[20,20]{1,0:T(8,128)S(1)} %convolution_multiply_fusion, s32[20]{0:T(128)S(1)} %or_bitcast_fusion), kind=kCustom, calls=%fused_computation | custom fusion | bytes 320 | tf_op jit(solution)/shard_map/jit(_diag)/jit(diagonal)/cond/branch_0_fun/gather | solution.py:387
  20.5 0.1 fusion.27
  20.6 0.1 fusion.24
  20.7 0.1 convert_convert_fusion
  20.8 0.0 copy-done.1
  20.8 0.0 copy-done
  20.8 0.3 fusion.chosen_ref
  21.2 0.1 pad_maximum_fusion.gram_ref
  21.3 14.1 %all-to-all-done = bf16[256,3,2,128]{3,2,1,0:T(2,128)(2,1)S(1)} async-done(((bf16[256,3,2,128]{3,2,1,0:T(2,128)(2,1)}), bf16[256,3,2,128]{3,2,1,0:T(2,128)(2,1)S(1)}, u32[]{:S(2)}, u32[]{:S(2)}) %all-to-all-start) | async-done | bytes 393248 | tf_op jit(solution)/shard_map/all_to_all | solution.py:349
  35.4 6.1 %main.1 = f32[256,128]{1,0:T(8,128)S(1)} custom-call(s32[1]{0:T(128)} %bitcast.me_ref, bf16[1536,128]{1,0:T(8,128)(2,1)S(1)} %bitcast.15, f32[20,768]{1,0:T(8,128)S(1)} %copy-done, f32[1,768]{1,0:T(1,128)S(1)} %broadcast_in_dim.6.gain_ref, bf16[72,768]{1,0:T(8,128)(2,1)S(1)} %get-tuple-element.15.parts_ref, ...), custom_call_target="tpu_custom_call" | custom-call | tf_op jit(solution)/shard_map/main/pallas_call | solution.py:337
  41.6 12.4 %all_to_all.20 = f32[32,8,128]{2,1,0:T(8,128)S(1)} all-to-all(f32[32,8,128]{2,1,0:T(8,128)S(1)} %bitcast.21), channel_id=1, replica_groups=mesh['layer'=8,'row'=4,'win'=8] {'row','win'}, dimensions={0} | all-to-all | bytes 262144 | tf_op jit(solution)/shard_map/all_to_all | solution.py:349
  53.9 0.1 relay.1
  54.0 9.6 %all_to_all.21 = f32[8,16,128]{2,1,0:T(8,128)S(1)} all-to-all(f32[8,16,128]{2,1,0:T(8,128)S(1)} %bitcast.22), channel_id=1, replica_groups=mesh['layer'=8,'row'=4,'win'=8] {'layer'}, dimensions={0} | all-to-all | bytes 131072 | tf_op jit(solution)/shard_map/all_to_all | solution.py:349
  63.6 0.1 total.1
  63.7 12.5 %all_to_all.22 = f32[32,8,128]{2,1,0:T(8,128)S(1)} all-to-all(f32[32,8,128]{2,1,0:T(8,128)S(1)} %bitcast.20), channel_id=1, replica_groups=mesh['layer'=8,'row'=4,'win'=8] {'row','win'}, dimensions={0} | all-to-all | bytes 262144 | tf_op jit(solution)/shard_map/all_to_all | solution.py:349
  76.2 0.8 %finish.1 = (f32[15,768]{1,0:T(8,128)}, f32[20,768]{1,0:T(8,128)}, f32[768]{0:T(1024)}) custom-call(f32[128,128]{1,0:T(8,128)S(1)} %bitcast.17, f32[256,128]{1,0:T(8,128)S(1)} %bitcast.18), custom_call_target="tpu_custom_call" | custom-call | tf_op jit(solution)/shard_map/finish/pallas_call | solution.py:337
  (11 shorter events, 0.1 us)
Async XLA Ops:
  0.6 20.2 %copy-start = (f32[20,768]{1,0:T(8,128)S(1)}, f32[20,768]{1,0:T(8,128)}, u32[]{:S(2)}) copy-start(f32[20,768]{1,0:T(8,128)} %stem_ref.1) | copy-start | bytes 184324
  0.6 20.1 %copy-start.1 = (f32[768]{0:T(1024)S(1)}, f32[768]{0:T(1024)}, u32[]{:S(2)}) copy-start(f32[768]{0:T(1024)} %param.7) | copy-start | bytes 9220
  2.6 32.8 %all-to-all-start = ((bf16[256,3,2,128]{3,2,1,0:T(2,128)(2,1)}), bf16[256,3,2,128]{3,2,1,0:T(2,128)(2,1)S(1)}, u32[]{:S(2)}, u32[]{:S(2)}) async-start(bf16[256,3,2,128]{3,2,1,0:T(2,128)(2,1)} %bitcast.23), calls=%async_computation | async-start | bytes 786432 | tf_op jit(solution)/shard_map/all_to_all | solution.py:349

commit v9 on v8

--- a/solution.py
+++ b/solution.py
@@ -29,6 +29,15 @@
         top = x.astype(BF16)
         out.append(top)
         x = x - top.astype(F32)
+    return out
+
+
+def outer_pieces(x, count):
+    out = []
+    for _ in range(count):
+        top = lax.reduce_precision(x, 8, 7)
+        out.append(top.astype(BF16))
+        x = x - top
     return out
 
 
@@ -378,7 +387,7 @@
     got = exchange(sent.reshape(n, LINE // 2, 2, half), AXES).reshape(LINE * n, half)
 
     parts, gained = [
-        jnp.concatenate([jnp.pad(part, ((0, 4), (0, 0))) for part in pieces(x, 3)], axis=0)
+        jnp.concatenate([jnp.pad(part, ((0, 4), (0, 0))) for part in outer_pieces(x, 3)], axis=0)
         for x in (stem_weight, stem_weight * norm_gain)
     ]
     gram = jnp.dot(stem_weight, stem_weight.T, precision=HIGH) * (1.0 / channels)
@@ -389,7 +398,7 @@
     odd = gram * (2.0 * ahead.T + same) + square * ((tap[:, None] == 1) & (tap[None] == 0))
     even, odd = jnp.pad(even[:16], ((0, 0), (0, 4))), jnp.pad(odd[4:], ((0, 0), (4, 0)))
     gram = jnp.concatenate([even, odd], axis=0)
-    gram = jnp.concatenate([part.astype(F32) for part in pieces(gram, 3)], axis=1)
+    gram = jnp.concatenate([part.astype(F32) for part in outer_pieces(gram, 3)], axis=1)
     row = jnp.arange(KW * channels, dtype=jnp.int32)[None, :]
     chosen = (row // share == jnp.arange(n, dtype=jnp.int32)[:, None]).astype(BF16)
     turn = (row % share == jnp.arange(ROWS, dtype=jnp.int32)[:, None]).astype(F32)

time: 77.4 us -> 77.4 us (level)
  waiting for transfers between devices: 14.1 us -> 12.6 us
  other arithmetic: 0.85 us -> 1.67 us
    all_to_all x1, waiting for transfers between devices: 14.1 us -> 12.6 us  [exchange(): return lax.all_to_all(x, axes, 0, 0, tiled=True)]
    convert_element_type x3 -> x2, other arithmetic: 0.18 us -> 1.01 us  [outer_pieces(): out.append(top.astype(BF16))]
  transfers between devices with their start and end apart: 1 -> 1, of which waited for: 1 -> 1; matrix products, arithmetic and copies ran while one was open for 4% -> 6% of each run, Pallas kernels for 0% -> 0%
where the time goes in v9:
time: 77.4 us; the launch traced here: 77 us
  blocking collectives  34.5 us (45%)
  starting transfers between devices  15.7 us (20%)
  waiting for transfers between devices  12.6 us (16%)
  Pallas kernels  9.06 us (12%)
  other arithmetic  1.67 us (2%)
  local copies, waits for them, and re-layouts  1.63 us (2%)
  matrix products  1.16 us (1%)
    all_to_all x3, blocking collectives, exchange(): return lax.all_to_all(x, axes, 0, 0, tiled=True)  34.5 us
    all_to_all x1, starting transfers between devices, exchange(): return lax.all_to_all(x, axes, 0, 0, tiled=True)  15.7 us
    all_to_all x1, waiting for transfers between devices, exchange(): return lax.all_to_all(x, axes, 0, 0, tiled=True)  12.6 us
    pallas_call x5, Pallas kernels, call(): pl.pallas_call(kernel, name=name, out_shape=out, in_specs=specs, out_spec...  9.06 us
  transfers between devices with their start and end apart: 1, of which 1 were waited for; matrix products, arithmetic and copies ran while one was open for 6% of the time, Pallas kernels for 0%

profile of v9, /device:TPU:1, one launch (start us, length us, event | category | flops | bytes accessed | tf_op | source)
XLA Modules:
  0.0 77.0 jit_solution(4435099228964714930)
XLA Ops:
  0.6 1.9 %pack.1 = bf16[1536,128]{1,0:T(8,128)(2,1)} custom-call(s32[1,256]{1,0:T(1,128)} %bases_hbm.1, bf16[15,768]{1,0:T(8,128)(2,1)} %weight_hbm.1, bf16[128,768]{1,0:T(8,128)(2,1)} %bitcast.24), custom_call_target="tpu_custom_call" | custom-call | tf_op jit(solution)/shard_map/pack/pallas_call | solution.py:346
  2.5 15.7 %all-to-all-start = ((bf16[256,3,2,128]{3,2,1,0:T(2,128)(2,1)}), bf16[256,3,2,128]{3,2,1,0:T(2,128)(2,1)S(1)}, u32[]{:S(2)}, u32[]{:S(2)}) async-start(bf16[256,3,2,128]{3,2,1,0:T(2,128)(2,1)} %bitcast.23), calls=%async_computation | async-start | bytes 786432 | tf_op jit(solution)/shard_map/all_to_all | solution.py:358
  18.3 0.1 fusion.28
  18.4 0.0 copy-start
  18.4 0.1 compare_convert_fusion
  18.5 0.7 broadcast_in_dim.6.gain_ref
  19.1 1.2 %convolution_multiply_fusion = f32[20,20]{1,0:T(8,128)S(1)} fusion(f32[20,768]{1,0:T(8,128)} %stem_ref.1), kind=kOutput, calls=%fused_computation.3 | convolution fusion | flops 3686800 | bytes 63040 | tf_op jit(solution)/shard_map/dot_general | solution.py:393
  20.3 0.9 %reduce-precision_convert_fusion.1 = (bf16[20,768]{1,0:T(8,128)(2,1)S(1)}, bf16[20,768]{1,0:T(8,128)(2,1)S(1)}, bf16[20,768]{1,0:T(8,128)(2,1)S(1)}, bf16[20,768...) fusion(f32[20,768]{1,0:T(8,128)} %stem_ref.1, f32[768]{0:T(1024)} %param.7), kind=kLoop, calls=%fused_computation.24 | loop fusion | flops 261120 | bytes 248832 | tf_op jit(solution)/shard_map/convert_element_type | solution.py:39
  21.2 0.1 slice.16
  21.3 0.3 fusion.chosen_ref
  21.7 0.8 %gather_fusion = f32[20]{0:T(128)S(1)} fusion(f32[20,20]{1,0:T(8,128)S(1)} %convolution_multiply_fusion, s32[20]{0:T(128)S(1)} %or_bitcast_fusion), kind=kCustom, calls=%fused_computation | custom fusion | bytes 320 | tf_op jit(solution)/shard_map/jit(_diag)/jit(diagonal)/cond/branch_0_fun/gather | solution.py:396
  22.5 0.1 fusion.27
  22.5 0.1 reduce-precision_convert_fusion.5
  22.6 0.1 maximum_convert_fusion.gram_ref
  22.8 12.6 %all-to-all-done = bf16[256,3,2,128]{3,2,1,0:T(2,128)(2,1)S(1)} async-done(((bf16[256,3,2,128]{3,2,1,0:T(2,128)(2,1)}), bf16[256,3,2,128]{3,2,1,0:T(2,128)(2,1)S(1)}, u32[]{:S(2)}, u32[]{:S(2)}) %all-to-all-start) | async-done | bytes 393248 | tf_op jit(solution)/shard_map/all_to_all | solution.py:358
  35.4 0.0 copy-done
  35.4 6.1 %main.1 = f32[256,128]{1,0:T(8,128)S(1)} custom-call(s32[1]{0:T(128)} %bitcast.me_ref, bf16[1536,128]{1,0:T(8,128)(2,1)S(1)} %bitcast.15, f32[20,768]{1,0:T(8,128)S(1)} %copy-done, f32[1,768]{1,0:T(1,128)S(1)} %broadcast_in_dim.6.gain_ref, bf16[72,768]{1,0:T(8,128)(2,1)S(1)} %get-tuple-element.16.parts_ref, ...), custom_call_target="tpu_custom_call" | custom-call | tf_op jit(solution)/shard_map/main/pallas_call | solution.py:346
  41.5 12.4 %all_to_all.20 = f32[32,8,128]{2,1,0:T(8,128)S(1)} all-to-all(f32[32,8,128]{2,1,0:T(8,128)S(1)} %bitcast.21), channel_id=1, replica_groups=mesh['layer'=8,'row'=4,'win'=8] {'row','win'}, dimensions={0} | all-to-all | bytes 262144 | tf_op jit(solution)/shard_map/all_to_all | solution.py:358
  53.9 0.1 relay.1
  54.0 9.6 %all_to_all.21 = f32[8,16,128]{2,1,0:T(8,128)S(1)} all-to-all(f32[8,16,128]{2,1,0:T(8,128)S(1)} %bitcast.22), channel_id=1, replica_groups=mesh['layer'=8,'row'=4,'win'=8] {'layer'}, dimensions={0} | all-to-all | bytes 131072 | tf_op jit(solution)/shard_map/all_to_all | solution.py:358
  63.6 0.1 total.1
  63.6 12.5 %all_to_all.22 = f32[32,8,128]{2,1,0:T(8,128)S(1)} all-to-all(f32[32,8,128]{2,1,0:T(8,128)S(1)} %bitcast.20), channel_id=1, replica_groups=mesh['layer'=8,'row'=4,'win'=8] {'row','win'}, dimensions={0} | all-to-all | bytes 262144 | tf_op jit(solution)/shard_map/all_to_all | solution.py:358
  76.2 0.8 %finish.1 = (f32[15,768]{1,0:T(8,128)}, f32[20,768]{1,0:T(8,128)}, f32[768]{0:T(1024)}) custom-call(f32[128,128]{1,0:T(8,128)S(1)} %bitcast.17, f32[256,128]{1,0:T(8,128)S(1)} %bitcast.18), custom_call_target="tpu_custom_call" | custom-call | tf_op jit(solution)/shard_map/finish/pallas_call | solution.py:346
  (9 shorter events, 0.1 us)
Async XLA Ops:
  2.5 32.8 %all-to-all-start = ((bf16[256,3,2,128]{3,2,1,0:T(2,128)(2,1)}), bf16[256,3,2,128]{3,2,1,0:T(2,128)(2,1)S(1)}, u32[]{:S(2)}, u32[]{:S(2)}) async-start(bf16[256,3,2,128]{3,2,1,0:T(2,128)(2,1)} %bitcast.23), calls=%async_computation | async-start | bytes 786432 | tf_op jit(solution)/shard_map/all_to_all | solution.py:358
  18.4 17.0 %copy-start = (f32[20,768]{1,0:T(8,128)S(1)}, f32[20,768]{1,0:T(8,128)}, u32[]{:S(2)}) copy-start(f32[20,768]{1,0:T(8,128)} %stem_ref.1) | copy-start | bytes 184324

commit v10 on v9

--- a/solution.py
+++ b/solution.py
@@ -18,6 +18,7 @@
 CUBE = 0.044715
 ROWS, SUMS, LINE = 16, TAPS + 1, 6
 CELLS = 2
+PARTS = 2
 LAG = 1
 LAYERS = 8
 NN, NT = (((1,), (0,)), ((), ())), (((1,), (1,)), ((), ()))
@@ -58,38 +59,46 @@
     return (1.0 + th) * (1.0 + (1.0 - th) * (x * (ROOT + (3.0 * ROOT * CUBE) * sq)))
 
 
-def pack_kernel(n, bases_hbm, weight_hbm, cot_hbm, out_ref, bases_ref, weight_ref, cot_ref, hold, sems):
-    copies = [
-        pltpu.make_async_copy(*pair, sems.at[i])
-        for i, pair in enumerate(
-            ((cot_hbm, cot_ref), (weight_hbm, weight_ref), (bases_hbm, bases_ref))
-        )
-    ]
+def pack_kernel(
+    n, bases_hbm, weight_hbm, cot_hbm, out_hbm, bases_ref, weight_ref, cot_ref, hold, out_ref, sems
+):
+    pairs = ((bases_hbm, bases_ref), (weight_hbm, weight_ref), (cot_hbm, cot_ref))
+    copies = [pltpu.make_async_copy(*pair, sems.at[i]) for i, pair in enumerate(pairs)]
     for copy in copies:
         copy.start()
-    for copy in copies:
-        copy.wait()
     half = cot_ref.shape[0]
     share, channels = weight_ref.shape
     cols = channels // n
-    for m in range(cols):
-        hold[pl.ds(m, n, stride=LINE), :] = cot_ref[:, m * n : (m + 1) * n].astype(F32).T
     count = 2 * half
     place = lax.broadcasted_iota(jnp.int32, (count, count), 0)
     lane = lax.broadcasted_iota(jnp.int32, (count, count), 1)
     wanted = jnp.where(lane < half, 2 * lane, 2 * (lane - half) + 1)
     pick = (place == wanted).astype(BF16)
+    copies[0].wait()
     row = bases_ref[...].astype(F32).astype(BF16)
     split = dot(jnp.broadcast_to(row, (8, count)), pick, NN)
     hold[pl.ds(3, n, stride=LINE), :] = jnp.broadcast_to(split[0:1, :half], (n, half))
     hold[pl.ds(4, n, stride=LINE), :] = jnp.broadcast_to(split[0:1, half:], (n, half))
+    copies[1].wait()
     weight = weight_ref[...].astype(F32)
     rows = []
     for m in range(cols):
         rows += [weight[:, m * n : (m + 1) * n], jnp.zeros((ROWS - share, n), F32)]
     rows.append(jnp.zeros((half - cols * ROWS, n), F32))
     hold[pl.ds(5, n, stride=LINE), :] = jnp.concatenate(rows, axis=0).T
-    out_ref[...] = hold[...].astype(BF16)
+    copies[2].wait()
+    part = n // PARTS
+    for i in range(PARTS):
+        for m in range(cols):
+            at = m * n + i * part
+            cell = cot_ref[:, at : at + part].astype(F32).T
+            hold[pl.ds(LINE * part * i + m, part, stride=LINE), :] = cell
+        lines = slice(LINE * part * i, LINE * part * (i + 1))
+        out_ref[lines, :] = hold[lines, :].astype(BF16)
+        copies.append(pltpu.make_async_copy(out_ref.at[lines], out_hbm.at[lines], sems.at[3 + i]))
+        copies[-1].start()
+    for copy in copies[3:]:
+        copy.wait()
 
 
 def main_kernel(
@@ -181,12 +190,13 @@
                     for parity in range(2)
                 ]
                 hots[i].append(jnp.where(sub < 4, *pair))
-        hots = [jnp.maximum(1.0 - jnp.abs(jnp.concatenate(x, axis=1) - base), 0.0) for x in hots]
-        return jnp.concatenate(dr, axis=1), jnp.concatenate(hots, axis=0)
+        hots = [jnp.concatenate(x, axis=1) - base for x in hots]
+        hots = jnp.maximum(1.0 - jnp.abs(jnp.concatenate(hots, axis=0).astype(BF16)), 0.0)
+        return jnp.concatenate(dr, axis=1), hots
 
     def look(cell):
-        dr, hots = cell
-        narrow = hots.astype(BF16)
+        dr, narrow = cell
+        hots = narrow.astype(F32)
         looked = dot(table, jnp.concatenate([narrow] * 3, axis=0), NN)
         taps = [looked[8 * t : 8 * t + 8] for t in range(KW)]
         mean_e = looked[40:48] * hots[0:8] + looked[48:56] * hots[8:16]
@@ -338,11 +348,11 @@
         gain_ref[lanes] = small[SUMS * m + TAPS]
 
 
-def call(kernel, name, out, operands, scratch=(), smem=0, space=pltpu.VMEM, limit=48):
+def call(kernel, name, out, operands, scratch=(), smem=0, space=pltpu.VMEM, out_space=pltpu.VMEM, limit=48):
     specs = [pl.BlockSpec(memory_space=pltpu.SMEM)] * smem
     specs += [pl.BlockSpec(memory_space=space)] * (len(operands) - smem)
     many = isinstance(out, tuple)
-    spec = pl.BlockSpec(memory_space=pltpu.VMEM)
+    spec = pl.BlockSpec(memory_space=out_space)
     return pl.pallas_call(
         kernel,
         name=name,
@@ -379,9 +389,11 @@
             pltpu.VMEM(conv_weight.shape, BF16),
             pltpu.VMEM(cotangent.shape[1:], BF16),
             pltpu.VMEM((LINE * n, half), F32),
-            pltpu.SemaphoreType.DMA((3,)),
+            pltpu.VMEM((LINE * n, half), BF16),
+            pltpu.SemaphoreType.DMA((3 + PARTS,)),
         ],
         space=pltpu.HBM,
+        out_space=pltpu.HBM,
         limit=60,
     )
     got = exchange(sent.reshape(n, LINE // 2, 2, half), AXES).reshape(LINE * n, half)

time: 77.4 us -> 77.4 us (level)
  no operation moved by 1% of the time
where the time goes in v10:
time: 77.4 us; the launch traced here: 77 us
  blocking collectives  34.5 us (45%)
  starting transfers between devices  15.7 us (20%)
  waiting for transfers between devices  12.6 us (16%)
  Pallas kernels  9.03 us (12%)
  other arithmetic  1.67 us (2%)
  local copies, waits for them, and re-layouts  1.63 us (2%)
  matrix products  1.16 us (1%)
    all_to_all x3, blocking collectives, exchange(): return lax.all_to_all(x, axes, 0, 0, tiled=True)  34.5 us
    all_to_all x1, starting transfers between devices, exchange(): return lax.all_to_all(x, axes, 0, 0, tiled=True)  15.7 us
    all_to_all x1, waiting for transfers between devices, exchange(): return lax.all_to_all(x, axes, 0, 0, tiled=True)  12.6 us
    pallas_call x5, Pallas kernels, call(): pl.pallas_call(kernel, name=name, out_shape=out, in_specs=specs, out_spec...  9.03 us
  transfers between devices with their start and end apart: 1, of which 1 were waited for; matrix products, arithmetic and copies ran while one was open for 6% of the time, Pallas kernels for 0%

profile of v10, /device:TPU:1, one launch (start us, length us, event | category | flops | bytes accessed | tf_op | source)
XLA Modules:
  0.0 77.0 jit_solution(6568587661503164931)
XLA Ops:
  0.6 1.9 %pack.1 = bf16[1536,128]{1,0:T(8,128)(2,1)} custom-call(s32[1,256]{1,0:T(1,128)} %bases_hbm.1, bf16[15,768]{1,0:T(8,128)(2,1)} %weight_hbm.1, bf16[128,768]{1,0:T(8,128)(2,1)} %bitcast.24), custom_call_target="tpu_custom_call" | custom-call | tf_op jit(solution)/shard_map/pack/pallas_call | solution.py:356
  2.5 15.7 %all-to-all-start = ((bf16[256,3,2,128]{3,2,1,0:T(2,128)(2,1)}), bf16[256,3,2,128]{3,2,1,0:T(2,128)(2,1)S(1)}, u32[]{:S(2)}, u32[]{:S(2)}) async-start(bf16[256,3,2,128]{3,2,1,0:T(2,128)(2,1)} %bitcast.23), calls=%async_computation | async-start | bytes 786432 | tf_op jit(solution)/shard_map/all_to_all | solution.py:368
  18.2 0.1 fusion.28
  18.3 0.0 copy-start
  18.3 0.1 compare_convert_fusion
  18.4 0.7 broadcast_in_dim.6.gain_ref
  19.1 1.2 %convolution_multiply_fusion = f32[20,20]{1,0:T(8,128)S(1)} fusion(f32[20,768]{1,0:T(8,128)} %stem_ref.1), kind=kOutput, calls=%fused_computation.3 | convolution fusion | flops 3686800 | bytes 63040 | tf_op jit(solution)/shard_map/dot_general | solution.py:405
  20.3 0.9 %reduce-precision_convert_fusion.1 = (bf16[20,768]{1,0:T(8,128)(2,1)S(1)}, bf16[20,768]{1,0:T(8,128)(2,1)S(1)}, bf16[20,768]{1,0:T(8,128)(2,1)S(1)}, bf16[20,768...) fusion(f32[20,768]{1,0:T(8,128)} %stem_ref.1, f32[768]{0:T(1024)} %param.7), kind=kLoop, calls=%fused_computation.24 | loop fusion | flops 261120 | bytes 248832 | tf_op jit(solution)/shard_map/convert_element_type | solution.py:40
  21.2 0.1 slice.16
  21.3 0.3 fusion.chosen_ref
  21.7 0.8 %gather_fusion = f32[20]{0:T(128)S(1)} fusion(f32[20,20]{1,0:T(8,128)S(1)} %convolution_multiply_fusion, s32[20]{0:T(128)S(1)} %or_bitcast_fusion), kind=kCustom, calls=%fused_computation | custom fusion | bytes 320 | tf_op jit(solution)/shard_map/jit(_diag)/jit(diagonal)/cond/branch_0_fun/gather | solution.py:408
  22.4 0.1 fusion.27
  22.5 0.1 reduce-precision_convert_fusion.5
  22.6 0.1 maximum_convert_fusion.gram_ref
  22.7 12.6 %all-to-all-done = bf16[256,3,2,128]{3,2,1,0:T(2,128)(2,1)S(1)} async-done(((bf16[256,3,2,128]{3,2,1,0:T(2,128)(2,1)}), bf16[256,3,2,128]{3,2,1,0:T(2,128)(2,1)S(1)}, u32[]{:S(2)}, u32[]{:S(2)}) %all-to-all-start) | async-done | bytes 393248 | tf_op jit(solution)/shard_map/all_to_all | solution.py:368
  35.3 0.0 copy-done
  35.3 6.1 %main.1 = f32[256,128]{1,0:T(8,128)S(1)} custom-call(s32[1]{0:T(128)} %bitcast.me_ref, bf16[1536,128]{1,0:T(8,128)(2,1)S(1)} %bitcast.15, f32[20,768]{1,0:T(8,128)S(1)} %copy-done, f32[1,768]{1,0:T(1,128)S(1)} %broadcast_in_dim.6.gain_ref, bf16[72,768]{1,0:T(8,128)(2,1)S(1)} %get-tuple-element.16.parts_ref, ...), custom_call_target="tpu_custom_call" | custom-call | tf_op jit(solution)/shard_map/main/pallas_call | solution.py:356
  41.5 12.4 %all_to_all.20 = f32[32,8,128]{2,1,0:T(8,128)S(1)} all-to-all(f32[32,8,128]{2,1,0:T(8,128)S(1)} %bitcast.21), channel_id=1, replica_groups=mesh['layer'=8,'row'=4,'win'=8] {'row','win'}, dimensions={0} | all-to-all | bytes 262144 | tf_op jit(solution)/shard_map/all_to_all | solution.py:368
  53.8 0.1 relay.1
  54.0 9.6 %all_to_all.21 = f32[8,16,128]{2,1,0:T(8,128)S(1)} all-to-all(f32[8,16,128]{2,1,0:T(8,128)S(1)} %bitcast.22), channel_id=1, replica_groups=mesh['layer'=8,'row'=4,'win'=8] {'layer'}, dimensions={0} | all-to-all | bytes 131072 | tf_op jit(solution)/shard_map/all_to_all | solution.py:368
  63.5 0.1 total.1
  63.6 12.5 %all_to_all.22 = f32[32,8,128]{2,1,0:T(8,128)S(1)} all-to-all(f32[32,8,128]{2,1,0:T(8,128)S(1)} %bitcast.20), channel_id=1, replica_groups=mesh['layer'=8,'row'=4,'win'=8] {'row','win'}, dimensions={0} | all-to-all | bytes 262144 | tf_op jit(solution)/shard_map/all_to_all | solution.py:368
  76.2 0.8 %finish.1 = (f32[15,768]{1,0:T(8,128)}, f32[20,768]{1,0:T(8,128)}, f32[768]{0:T(1024)}) custom-call(f32[128,128]{1,0:T(8,128)S(1)} %bitcast.17, f32[256,128]{1,0:T(8,128)S(1)} %bitcast.18), custom_call_target="tpu_custom_call" | custom-call | tf_op jit(solution)/shard_map/finish/pallas_call | solution.py:356
  (9 shorter events, 0.1 us)
Async XLA Ops:
  2.5 32.8 %all-to-all-start = ((bf16[256,3,2,128]{3,2,1,0:T(2,128)(2,1)}), bf16[256,3,2,128]{3,2,1,0:T(2,128)(2,1)S(1)}, u32[]{:S(2)}, u32[]{:S(2)}) async-start(bf16[256,3,2,128]{3,2,1,0:T(2,128)(2,1)} %bitcast.23), calls=%async_computation | async-start | bytes 786432 | tf_op jit(solution)/shard_map/all_to_all | solution.py:368
  18.3 17.0 %copy-start = (f32[20,768]{1,0:T(8,128)S(1)}, f32[20,768]{1,0:T(8,128)}, u32[]{:S(2)}) copy-start(f32[20,768]{1,0:T(8,128)} %stem_ref.1) | copy-start | bytes 184324
